TPU v7x, 128 devices: a whole 4x4x4 slice. The times are simulated.
128 devices in a mesh: gx: 8 (over x, core), gy: 16 (over y, z).
Axes of the slice: x: 4, y: 4, z: 4, core: 2. Of those that a mesh axis runs over, the one named last changes fastest.
Arguments:
- state_before: float32 [768, 5, 32768], P(('gx', 'gy')), as said below
- before_start: int32 [8, 16], replicated, may hold values from 0 to 61, as said below
- after_start: int32 [8, 16], replicated, may hold values from 0 to 61, as said below
- time_step: float32 [], replicated, may hold values from 0.02 to 0.03
Outputs:
- state_after: float32 [768, 5, 32768], P(('gx', 'gy'))
- added_mass: float32 [], replicated
Inputs may be any that keep to these rules, and one draw needn't show every extreme that they name: state_before has density in 0.2 to 5, velocity components in -1 to 1 and pressure in 0.5 to 2; slots past an owner's blocks are read by no output. before_start[g, 0] = 0 and before_start[g, k] lies within 1 of k * 4; in every x-slab one entry is k * 4 + 1 and another k * 4 - 1; in x-slab 0 the last entry is (15) * 4 + 1. after_start[g, 0] = 0 and after_start[g, k] lies within 1 of k * 4; in every x-slab one entry is k * 4 + 1 and another k * 4 - 1; in x-slab 0 the last entry is (15) * 4 + 1.
All inputs are finite; a program needn't handle non-finite values.
Results may differ from a plain program's by a relative error of at most 0.0003.
Values sent between devices are 32-bit elements; how exact they have to be, the bound alone decides.
A program may use at most 128 MiB of HBM per device.

v0:
```python
import jax
import jax.numpy as jnp
import numpy as np
from jax import lax
from jax.experimental import pallas as pl
from jax.experimental.pallas import tpu as pltpu
from jax.sharding import PartitionSpec as P

GAMMA = 5.0 / 3.0
FLOOR = 0.25
MESH = pl.DeviceIdType.MESH
HIGHEST = lax.Precision.HIGHEST

NK, NG = 16, 8


def tables():
    def sine(n):
        i = np.arange(1, n + 1)
        return np.sin(np.pi * ((i[:, None] * i[None, :]) % (2 * (n + 1))) / (n + 1))

    sine_y, sine_z = sine(512), sine(64)
    forward = np.zeros((16, 2, 4, 2, 64))
    for u in range(2):
        forward[:, u, :, u, :] = sine_z.reshape(16, 4, 64)
    forward = forward.reshape(128, 128)
    order = np.arange(512).reshape(16, 8, 4).transpose(0, 2, 1).reshape(512)
    ordered = sine_y[order]
    modes_y = 2 - 2 * np.cos(np.pi * np.arange(1, 513) / 513)
    modes_z = 2 - 2 * np.cos(np.pi * np.arange(1, 65) / 65)
    h = 0.5 * (modes_z[:, None] + modes_y[None, :])
    root = np.sqrt(h * (h + 2))
    lam = 1 / (1 + h + root)
    gain = -0.5 / root

    def rows(values):
        return np.broadcast_to(values.reshape(16, 1, 4, 512), (16, 2, 4, 512)).reshape(16, 8, 512)

    table = np.stack([rows(lam), rows(gain)], axis=1)
    f32 = np.float32
    return (
        (forward * (4.0 / 64)).astype(f32),
        (forward * (2.0 / 65)).astype(f32),
        ordered.astype(f32),
        np.ascontiguousarray(ordered.T * (2.0 / 513)).astype(f32),
        table.astype(f32),
    )


def lanes():
    return lax.broadcasted_iota(jnp.int32, (8, 128), 1)


def swap4(parts):
    group = lanes() // 32
    low, even = group < 2, group % 2 == 0
    a, b, c, d = parts
    a, c = jnp.where(low, a, pltpu.roll(c, 64, 1)), jnp.where(low, pltpu.roll(a, 64, 1), c)
    b, d = jnp.where(low, b, pltpu.roll(d, 64, 1)), jnp.where(low, pltpu.roll(b, 64, 1), d)
    a, b = jnp.where(even, a, pltpu.roll(b, 32, 1)), jnp.where(even, pltpu.roll(a, 96, 1), b)
    c, d = jnp.where(even, c, pltpu.roll(d, 32, 1)), jnp.where(even, pltpu.roll(c, 96, 1), d)
    return a, b, c, d


def half_slope(down, up):
    quarter = 0.25 * (down + up)
    low = jnp.minimum(jnp.maximum(down, up), 0.0)
    high = jnp.maximum(jnp.minimum(down, up), 0.0)
    return jnp.minimum(jnp.maximum(quarter, low), high)


def face_flux(left, right, normal):
    def side(w):
        rho, vx, vy, vz, p = w
        gp = GAMMA * p
        return gp * lax.rsqrt(gp * rho), 0.5 * (vx * vx + vy * vy + vz * vz)

    sound_l, half_l = side(left)
    sound_r, half_r = side(right)
    ul, ur = left[1 + normal], right[1 + normal]
    fast = jnp.maximum(jnp.maximum(ul + sound_l, ur + sound_r), 0.0)
    slow = jnp.minimum(jnp.minimum(ul - sound_l, ur - sound_r), 0.0)
    inverse = 1.0 / (fast - slow)
    a, b = fast * inverse, slow * inverse
    d = fast * b
    kl, kr = a * ul - d, d - b * ur
    gl, gr = left[0] * kl, right[0] * kr
    apl, bpr = a * left[4], b * right[4]
    out = [gl + gr]
    for i in range(3):
        term = gl * left[1 + i] + gr * right[1 + i]
        out.append(term + (apl - bpr) if i == normal else term)
    out.append(
        1.5 * (left[4] * kl + right[4] * kr) + (gl * half_l + gr * half_r) + (apl * ul - bpr * ur)
    )
    return out


def cell_flux(w, normal):
    rho, p, u = w[0], w[4], w[1 + normal]
    mass = rho * u
    out = [mass]
    for i in range(3):
        out.append(mass * w[1 + i] + p if i == normal else mass * w[1 + i])
    half = 0.5 * (w[1] * w[1] + w[2] * w[2] + w[3] * w[3])
    out.append(2.5 * p * u + mass * half)
    return out


def at8(row):
    return pl.ds(pl.multiple_of(row, 8), 8)


EDGE, REST, HALO, PHI, AFTER, A2A, BACK, MOM, DEF_Y, DEF_X, N_SEM = (
    0, 2, 4, 8, 12, 14, 30, 46, 54, 70, 78,
)


def step_kernel(
    st, before, dt_ref, bz_h, bzi_h, sf_h, si_h, tab_h,
    nb, added,
    raw, tmp, dense, tail, next_head, prev_tail, cons, prim, acc, pot, pot0,
    xs, xr, ys, yr, pxs, pxr, pys, pyr,
    spec_t, spec_r, lines, trans, vsol, back_t, back_r, mom, defs, dgx,
    bz, bzi, sf, si, tab, load_sem, ss, rs,
):
    g, k = lax.axis_index("gx"), lax.axis_index("gy")
    k_up, k_dn = (k + 1) % NK, (k + NK - 1) % NK
    g_up, g_dn = (g + 1) % NG, (g + NG - 1) % NG
    dt = dt_ref[0, 0]
    lane = lanes()
    sub = lax.broadcasted_iota(jnp.int32, (8, 128), 0)
    zed = lane % 64

    loads = [pltpu.make_async_copy(st.at[f], raw.at[f], load_sem.at[f]) for f in range(5)]
    consts = [(bz_h, bz), (sf_h, sf), (tab_h.at[k], tab), (si_h, si), (bzi_h, bzi)]
    const_loads = [
        pltpu.make_async_copy(a, b, load_sem.at[5 + i]) for i, (a, b) in enumerate(consts)
    ]
    for c in loads + const_loads:
        c.start()

    barrier = pltpu.get_barrier_semaphore()

    def greet_y(o, _):
        pl.semaphore_signal(barrier, inc=1, device_id={"gy": (k + o) % NK}, device_id_type=MESH)
        return 0

    def greet_x(o, _):
        pl.semaphore_signal(barrier, inc=1, device_id={"gx": (g + o) % NG}, device_id_type=MESH)
        return 0

    lax.fori_loop(1, NK, greet_y, 0)
    lax.fori_loop(1, NG, greet_x, 0)

    def send(src, dst, sem, device, rsem=None):
        return pltpu.make_async_remote_copy(
            src_ref=src, dst_ref=dst, send_sem=ss.at[sem], recv_sem=rs.at[sem if rsem is None else rsem],
            device_id=device, device_id_type=MESH,
        )

    begin = before[g, k]
    end = jnp.where(k < NK - 1, before[g, jnp.minimum(k + 1, NK - 1)], 4 * NK)
    lead, trail = jnp.clip(begin - 4 * k, -1, 1), jnp.clip(end - 4 * (k + 1), -1, 1)
    last = jnp.clip(end - begin - 1, 0, 5)

    def spread(f):
        def body(x4, _):
            for i4 in range(4):
                x = x4 * 4 + i4
                v = raw[f, :, pl.ds(pl.multiple_of(x * 1024, 1024), 1024)]
                for s in range(8):
                    tmp[i4, 8 * s : 8 * s + 6, :] = v[:, 128 * s : 128 * s + 128]
                for slot in range(6):
                    dense[slot, f, x] = tmp[i4, pl.ds(slot, 8, stride=8), :]
            return 0

        lax.fori_loop(0, 8, body, 0)

        def tails(x4, _):
            for i4 in range(4):
                tail[f, x4 * 4 + i4] = dense[last, f, x4 * 4 + i4]
            return 0

        lax.fori_loop(0, 8, tails, 0)

    def assemble(f):
        def body(x, _):
            q0 = jnp.where(lead > 0, prev_tail[f, x], dense[jnp.maximum(-lead, 0), f, x])
            q1 = dense[1 - lead, f, x]
            q2 = dense[2 - lead, f, x]
            q3 = jnp.where(trail < 0, next_head[f, x], dense[3 - lead, f, x])
            for j, v in enumerate(swap4((q0, q2, q1, q3))):
                cons[f, at8(x * 32 + 8 * j), :] = v
            return 0

        lax.fori_loop(0, 32, body, 0, unroll=2)

    loads[0].wait()
    spread(0)
    pl.semaphore_wait(barrier, NK + NG - 2)
    edges = [
        send(dense.at[0, 0], next_head.at[0], EDGE, {"gy": k_dn}),
        send(tail.at[0], prev_tail.at[0], EDGE + 1, {"gy": k_up}),
    ]
    for c in edges:
        c.start()
    for f in range(1, 5):
        loads[f].wait()
        spread(f)
    for c in edges:
        c.wait_recv()
    assemble(0)
    for c in const_loads:
        c.wait()

    spec_t[...] = lax.dot_general(
        bz[...], cons[0], (((1,), (1,)), ((), ())),
        precision=HIGHEST, preferred_element_type=jnp.float32,
    )

    def a2a_copy(peer, source):
        return send(
            spec_t.at[at8(8 * peer), :], spec_r.at[source], A2A + peer, {"gy": peer}, A2A + source
        )

    def start_a2a(o, _):
        a2a_copy((k + o) % NK, k).start()
        return 0

    lax.fori_loop(1, NK, start_a2a, 0)
    spec_r[k] = spec_t[at8(8 * k), :]

    rest = [
        send(dense.at[0, pl.ds(1, 4)], next_head.at[pl.ds(1, 4)], REST, {"gy": k_dn}),
        send(tail.at[pl.ds(1, 4)], prev_tail.at[pl.ds(1, 4)], REST + 1, {"gy": k_up}),
    ]
    for c in rest:
        c.start()

    def wait_a2a(o, _):
        source = (k + NK - o) % NK
        a2a_copy(source, source).wait_recv()
        return 0

    lax.fori_loop(1, NK, wait_a2a, 0)

    def to_lines(x4, _):
        for m in range(4):
            parts = [
                spec_r[4 * m + b, :, pl.ds(pl.multiple_of(x4 * 128, 128), 128)] for b in range(4)
            ]
            for i, v in enumerate(swap4(parts)):
                lines[at8(x4 * 32 + 8 * i), 128 * m : 128 * m + 128] = v
        return 0

    lax.fori_loop(0, 8, to_lines, 0)
    trans[...] = jnp.dot(
        lines[...], sf[...], precision=HIGHEST, preferred_element_type=jnp.float32
    )

    lam, gain = tab[0], tab[1]
    lam2 = lam * lam
    lam4 = lam2 * lam2
    lam8 = lam4 * lam4
    lam16 = lam8 * lam8
    lam32 = lam16 * lam16
    lam64 = lam32 * lam32

    def sums(i, carry):
        u, v = carry
        return trans[at8(8 * i), :] + lam * u, trans[at8(8 * (31 - i)), :] + lam * v

    zero = jnp.zeros((8, 512), jnp.float32)
    up_sum, down_sum = lax.fori_loop(0, 32, sums, (zero, zero))
    upper = lax.broadcasted_iota(jnp.int32, (8, 512), 0) >= 4
    up_roll, down_roll = pltpu.roll(up_sum, 4, 0), pltpu.roll(down_sum, 4, 0)
    mom[g] = jnp.where(upper, up_sum + lam32 * up_roll, down_sum + lam32 * down_roll)

    def mom_copy(peer, source):
        return send(mom.at[source], mom.at[source], MOM + peer, {"gx": peer}, MOM + source)

    def start_mom(o, _):
        mom_copy((g + o) % NG, g).start()
        return 0

    lax.fori_loop(1, NG, start_mom, 0)

    for c in rest:
        c.wait_recv()
    for f in range(1, 5):
        assemble(f)

    def primitives(x, _):
        for j in range(4):
            rho, mx, my, mz, energy = [cons[f, at8(x * 32 + 8 * j), :] for f in range(5)]
            inverse = 1.0 / rho
            vx, vy, vz = mx * inverse, my * inverse, mz * inverse
            p = (GAMMA - 1.0) * (energy - 0.5 * rho * (vx * vx + vy * vy + vz * vz))
            for f, v in enumerate((rho, vx, vy, vz, p)):
                prim[f, at8((x + 2) * 64 + (j + 2) * 8), :] = v
        return 0

    lax.fori_loop(0, 32, primitives, 0)

    for f in range(5):
        for r in range(2):
            for j in range(4):
                row = f * 64 + r * 32 + j * 8
                xs[0, row : row + 8, :] = prim[f, (2 + r) * 64 + (j + 2) * 8 : (2 + r) * 64 + (j + 3) * 8, :]
                xs[1, row : row + 8, :] = prim[f, (32 + r) * 64 + (j + 2) * 8 : (32 + r) * 64 + (j + 3) * 8, :]
            for q in range(4):
                row = f * 64 + r * 32 + q * 8
                ys[0, row : row + 8, :] = prim[f, pl.ds((2 + 8 * q) * 64 + (2 + r) * 8, 8, stride=64), :]
                ys[1, row : row + 8, :] = prim[f, pl.ds((2 + 8 * q) * 64 + (4 + r) * 8 + 7, 8, stride=64), :]
    halo = [
        send(xs.at[0], xr.at[1], HALO, {"gx": g_dn}),
        send(xs.at[1], xr.at[0], HALO + 1, {"gx": g_up}),
        send(ys.at[0], yr.at[1], HALO + 2, {"gy": k_dn}),
        send(ys.at[1], yr.at[0], HALO + 3, {"gy": k_up}),
    ]
    for c in halo:
        c.start()

    def wait_mom(o, _):
        source = (g + NG - o) % NG
        mom_copy(source, source).wait_recv()
        return 0

    lax.fori_loop(1, NG, wait_mom, 0)
    from_low, from_high, at_start, at_end = zero, zero, zero, zero
    power_low, power_high = zero + 1.0, zero + 1.0
    for i in range(NG):
        m_up, m_dn = mom[i], mom[NG - 1 - i]
        ups = jnp.where(upper, m_up, pltpu.roll(m_up, 4, 0))
        downs = jnp.where(upper, pltpu.roll(m_dn, 4, 0), m_dn)
        from_low = jnp.where(i < g, from_low * lam64 + ups, from_low)
        from_high = jnp.where(NG - 1 - i > g, from_high * lam64 + downs, from_high)
        at_end = at_end * lam64 + ups
        at_start = at_start * lam64 + downs
        power_low = jnp.where(i < g, power_low * lam64, power_low)
        power_high = jnp.where(NG - 1 - i > g, power_high * lam64, power_high)
    lam128 = lam64 * lam64
    lam256 = lam128 * lam128
    whole = lam256 * lam256 * lam
    at_start, at_end = lam * at_start, lam * at_end
    scale = 1.0 / (1.0 - whole * whole)
    from_low = from_low - (at_start - whole * at_end) * scale * power_low
    from_high = from_high - (at_end - whole * at_start) * scale * power_high
    first_u = jnp.where(upper, up_roll + lam32 * from_low, from_low)
    first_v = jnp.where(upper, from_high, down_roll + lam32 * from_high)

    def downward(i, v):
        v = trans[at8(8 * (31 - i)), :] + lam * v
        vsol[at8(8 * (31 - i)), :] = v
        return v

    lax.fori_loop(0, 32, downward, first_v)

    def upward(i, u):
        carried = lam * u
        f = trans[at8(8 * i), :]
        trans[at8(8 * i), :] = gain * (carried + vsol[at8(8 * i), :])
        return f + carried

    lax.fori_loop(0, 32, upward, first_u)
    lines[...] = jnp.dot(
        trans[...], si[...], precision=HIGHEST, preferred_element_type=jnp.float32
    )

    def from_lines(x4, _):
        for m in range(4):
            parts = [lines[at8(x4 * 32 + 8 * i), 128 * m : 128 * m + 128] for i in range(4)]
            for b, v in enumerate(swap4(parts)):
                back_t[4 * m + b, :, pl.ds(pl.multiple_of(x4 * 128, 128), 128)] = v
        return 0

    lax.fori_loop(0, 8, from_lines, 0)

    def back_copy(peer, source):
        return send(
            back_t.at[peer], back_r.at[at8(8 * source), :], BACK + peer, {"gy": peer}, BACK + source
        )

    def start_back(o, _):
        back_copy((k + o) % NK, k).start()
        return 0

    lax.fori_loop(1, NK, start_back, 0)
    back_r[at8(8 * k), :] = back_t[k]

    def sweep_z(x, _):
        for j in range(4):
            w = [prim[f, at8((x + 2) * 64 + (j + 2) * 8), :] for f in range(5)]
            left, right = [], []
            for v in w:
                down = jnp.where(zed == 0, 0.0, v - pltpu.roll(v, 1, 1))
                up = jnp.where(zed == 63, 0.0, pltpu.roll(down, 127, 1))
                h = half_slope(down, up)
                left.append(v + h)
                lower = v - h
                right.append(jnp.where(zed == 63, lower, pltpu.roll(lower, 127, 1)))
            high = face_flux(left, right, 2)
            wall = cell_flux(w, 2)
            for f in range(5):
                low = jnp.where(zed == 0, wall[f], pltpu.roll(high[f], 1, 1))
                acc[f, at8((x + 1) * 32 + 8 * j), :] = high[f] - low
        return 0

    lax.fori_loop(0, 32, sweep_z, 0)

    for c in halo:
        c.wait_recv()

    for f in range(5):
        for r in range(2):
            for j in range(4):
                row = f * 64 + r * 32 + j * 8
                e = (j + 2) * 8

                def plane(xx):
                    return prim[f, (xx + 2) * 64 + e : (xx + 2) * 64 + e + 8, :]

                low = pltpu.roll(jnp.where(lane >= 64, xr[0, row : row + 8, :], plane(30 + r)), 64, 1)
                low = jnp.where((lane < 64) & (g == 0), plane(0), low)
                prim[f, r * 64 + e : r * 64 + e + 8, :] = low
                high = pltpu.roll(jnp.where(lane < 64, xr[1, row : row + 8, :], plane(r)), 64, 1)
                high = jnp.where((lane >= 64) & (g == NG - 1), plane(31), high)
                prim[f, (34 + r) * 64 + e : (34 + r) * 64 + e + 8, :] = high

    def place_y(x, _):
        base = (x + 2) * 64
        for f in range(5):
            rows = [prim[f, at8(base + 16 + 8 * j), :] for j in range(4)]
            first = jnp.broadcast_to(rows[0][0:1, :], (8, 128))
            final = jnp.broadcast_to(rows[3][7:8, :], (8, 128))
            for r in range(2):
                row = f * 64 + r * 32 + x
                low = jnp.where(k == 0, first, jnp.broadcast_to(yr[0, pl.ds(row, 1), :], (8, 128)))
                prim[f, at8(base + 8 * r), :] = jnp.where(sub == 0, low, pltpu.roll(rows[2 + r], 1, 0))
                high = jnp.where(k == NK - 1, final, jnp.broadcast_to(yr[1, pl.ds(row, 1), :], (8, 128)))
                prim[f, at8(base + 48 + 8 * r), :] = jnp.where(sub == 7, high, pltpu.roll(rows[r], 7, 0))
        return 0

    lax.fori_loop(0, 32, place_y, 0)

    def sweep_y(x, _):
        base = (x + 2) * 64
        previous_left, previous_flux = None, None
        for e in range(1, 7):
            left, right = [], []
            for f in range(5):
                v = prim[f, at8(base + 8 * e), :]
                down = v - prim[f, at8(base + 8 * e - 8), :]
                up = prim[f, at8(base + 8 * e + 8), :] - v
                h = half_slope(down, up)
                left.append(v + h)
                right.append(v - h)
            if previous_left is not None:
                flux = face_flux(previous_left, right, 1)
                if previous_flux is not None:
                    for f in range(5):
                        row = at8((x + 1) * 32 + 8 * (e - 3))
                        acc[f, row, :] = acc[f, row, :] + (flux[f] - previous_flux[f])
                previous_flux = flux
            previous_left = left
        return 0

    lax.fori_loop(0, 32, sweep_y, 0)

    def sweep_x(j, _):
        e = (j + 2) * 8

        def cell(f, i):
            return prim[f, at8((i + 2) * 64 + e), :]

        def body(i, carry):
            value, down, left, flux = carry
            new_value, new_down, new_left, right = [], [], [], []
            for f in range(5):
                v = cell(f, i + 1)
                up = v - value[f]
                h = half_slope(down[f], up)
                right.append(value[f] - h)
                new_left.append(value[f] + h)
                new_value.append(v)
                new_down.append(up)
            new_flux = face_flux(left, right, 0)
            for f in range(5):
                row = at8(i * 32 + 8 * j)
                acc[f, row, :] = acc[f, row, :] + (new_flux[f] - flux[f])
            return new_value, new_down, new_left, new_flux

        value, down, left, flux = [], [], [], []
        for f in range(5):
            a, b, c = cell(f, -2), cell(f, -1), cell(f, 0)
            left.append(b + half_slope(b - a, c - b))
            value.append(c)
            down.append(c - b)
            flux.append(jnp.zeros((8, 128), jnp.float32))
        lax.fori_loop(0, 33, body, (value, down, left, flux))
        return 0

    for f in range(5):
        acc[f, 0:32, :] = jnp.zeros((32, 128), jnp.float32)
    lax.fori_loop(0, 4, sweep_x, 0)

    def deficit(x, total):
        for j in range(4):
            new = cons[0, at8(x * 32 + 8 * j), :] - dt * acc[0, at8((x + 1) * 32 + 8 * j), :]
            total = total + (jnp.maximum(new, FLOOR) - new)
        return total

    defs[k] = lax.fori_loop(0, 32, deficit, jnp.zeros((8, 128), jnp.float32))

    def def_copy(peer, source):
        return send(defs.at[source], defs.at[source], DEF_Y + peer, {"gy": peer}, DEF_Y + source)

    def start_def(o, _):
        def_copy((k + o) % NK, k).start()
        return 0

    lax.fori_loop(1, NK, start_def, 0)

    def wait_back(o, _):
        source = (k + NK - o) % NK
        back_copy(source, source).wait_recv()
        return 0

    lax.fori_loop(1, NK, wait_back, 0)
    pot0[...] = lax.dot_general(
        back_r[...], bzi[...], (((0,), (0,)), ((), ())),
        precision=HIGHEST, preferred_element_type=jnp.float32,
    )
    pxs[0] = pot0[0:32, :]
    pxs[1] = pot0[31 * 32 : 32 * 32, :]
    for q in range(4):
        pys[0, 8 * q : 8 * q + 8, :] = pot0[pl.ds(8 * q * 32, 8, stride=32), :]
        pys[1, 8 * q : 8 * q + 8, :] = pot0[pl.ds(8 * q * 32 + 31, 8, stride=32), :]
    phi_halo = [
        send(pxs.at[0], pxr.at[1], PHI, {"gx": g_dn}),
        send(pxs.at[1], pxr.at[0], PHI + 1, {"gx": g_up}),
        send(pys.at[0], pyr.at[1], PHI + 2, {"gy": k_dn}),
        send(pys.at[1], pyr.at[0], PHI + 3, {"gy": k_up}),
    ]
    for c in phi_halo:
        c.start()

    def wait_def(o, _):
        source = (k + NK - o) % NK
        def_copy(source, source).wait_recv()
        return 0

    lax.fori_loop(1, NK, wait_def, 0)
    dgx[g] = jnp.sum(defs[...], axis=0)

    def dgx_copy(peer, source):
        return send(dgx.at[source], dgx.at[source], DEF_X + peer, {"gx": peer}, DEF_X + source)

    def start_dgx(o, _):
        dgx_copy((g + o) % NG, g).start()
        return 0

    lax.fori_loop(1, NG, start_dgx, 0)

    for c in phi_halo:
        c.wait_recv()
    for j in range(4):
        low = pltpu.roll(
            jnp.where(lane >= 64, pxr[0, 8 * j : 8 * j + 8, :], pot0[31 * 32 + 8 * j : 31 * 32 + 8 * j + 8, :]), 64, 1
        )
        pot[8 + 8 * j : 16 + 8 * j, :] = jnp.where((lane < 64) & (g == 0), 0.0, low)
        high = pltpu.roll(jnp.where(lane < 64, pxr[1, 8 * j : 8 * j + 8, :], pot0[8 * j : 8 * j + 8, :]), 64, 1)
        pot[33 * 48 + 8 + 8 * j : 33 * 48 + 16 + 8 * j, :] = jnp.where((lane >= 64) & (g == NG - 1), 0.0, high)

    def place_pot(x, _):
        base = (x + 1) * 48
        rows = [pot0[at8(x * 32 + 8 * j), :] for j in range(4)]
        for j in range(4):
            pot[at8(base + 8 + 8 * j), :] = rows[j]
        low = jnp.where(k == 0, 0.0, jnp.broadcast_to(pyr[0, pl.ds(x, 1), :], (8, 128)))
        pot[at8(base), :] = jnp.where(sub == 0, low, pltpu.roll(rows[3], 1, 0))
        high = jnp.where(k == NK - 1, 0.0, jnp.broadcast_to(pyr[1, pl.ds(x, 1), :], (8, 128)))
        pot[at8(base + 40), :] = jnp.where(sub == 7, high, pltpu.roll(rows[0], 7, 0))
        return 0

    lax.fori_loop(0, 32, place_pot, 0)

    def finish(x, _):
        base = (x + 1) * 48 + 8
        new = [[None] * 4 for _ in range(5)]
        for j in range(4):
            here = pot[at8(base + 8 * j), :]
            half = -0.5 * dt
            ax = half * (pot[at8(base + 48 + 8 * j), :] - pot[at8(base - 48 + 8 * j), :])
            ay = half * (pot[at8(base + 8 + 8 * j), :] - pot[at8(base - 8 + 8 * j), :])
            az = half * (
                jnp.where(zed == 63, 0.0, pltpu.roll(here, 127, 1))
                - jnp.where(zed == 0, 0.0, pltpu.roll(here, 1, 1))
            )
            u = [cons[f, at8(x * 32 + 8 * j), :] for f in range(5)]
            change = [acc[f, at8((x + 1) * 32 + 8 * j), :] for f in range(5)]
            new[0][j] = jnp.maximum(u[0] - dt * change[0], FLOOR)
            for i, a in enumerate((ax, ay, az)):
                new[1 + i][j] = u[1 + i] - dt * change[1 + i] + u[0] * a
            new[4][j] = u[4] - dt * change[4] + (u[1] * ax + u[2] * ay + u[3] * az)
        for f in range(5):
            b0, b2, b1, b3 = swap4(new[f])
            for q, v in enumerate((b0, b1, b2, b3)):
                nb[1 + q, f, x] = v
        return 0

    lax.fori_loop(0, 32, finish, 0)
    after = [
        send(nb.at[1], nb.at[5], AFTER, {"gy": k_dn}),
        send(nb.at[4], nb.at[0], AFTER + 1, {"gy": k_up}),
    ]
    for c in after:
        c.start()

    def wait_dgx(o, _):
        source = (g + NG - o) % NG
        dgx_copy(source, source).wait_recv()
        return 0

    lax.fori_loop(1, NG, wait_dgx, 0)
    added[0, 0] = jnp.sum(jnp.sum(dgx[...], axis=0)) * (1.0 / 512)

    for c in edges + rest + halo + phi_halo:
        c.wait_send()

    def sent_y(o, _):
        peer = (k + o) % NK
        a2a_copy(peer, k).wait_send()
        back_copy(peer, k).wait_send()
        def_copy(peer, k).wait_send()
        return 0

    def sent_x(o, _):
        peer = (g + o) % NG
        mom_copy(peer, g).wait_send()
        dgx_copy(peer, g).wait_send()
        return 0

    lax.fori_loop(1, NK, sent_y, 0)
    lax.fori_loop(1, NG, sent_x, 0)
    for c in after:
        c.wait()


def place_kernel(after, where, nb, out, tmp):
    g, k = where[0], where[1]
    begin = after[g, k]
    end = jnp.where(k < NK - 1, after[g, jnp.minimum(k + 1, NK - 1)], 4 * NK)
    lead, held = jnp.clip(begin - 4 * k, -1, 1), end - begin

    def body(x4, _):
        for i4 in range(4):
            x = x4 * 4 + i4
            for slot in range(6):
                index = jnp.minimum(slot + lead + 1, 5)
                v = jnp.where(slot < held, nb[index, 0, x], 0.0)
                tmp[i4, pl.ds(slot, 8, stride=8), :] = v
            for s in range(8):
                out[0, :, pl.ds(pl.multiple_of(x * 1024 + 128 * s, 128), 128)] = tmp[i4, 8 * s : 8 * s + 6, :]
        return 0

    lax.fori_loop(0, 8, body, 0)


def per_device(consts, state_before, before_start, after_start, time_step):
    f32 = jnp.float32
    st = jnp.transpose(state_before, (1, 0, 2))
    any_spec = pl.BlockSpec(memory_space=pl.ANY)
    smem = pl.BlockSpec(memory_space=pltpu.SMEM)
    vmem = pl.BlockSpec(memory_space=pltpu.VMEM)
    block = (5, 32, 8, 128)

    def scratch(*shape):
        return pltpu.VMEM(shape, f32)

    nb, added = pl.pallas_call(
        step_kernel,
        out_shape=(jax.ShapeDtypeStruct((6,) + block, f32), jax.ShapeDtypeStruct((1, 1), f32)),
        in_specs=[any_spec, smem, smem] + [any_spec] * 5,
        out_specs=(vmem, smem),
        scratch_shapes=[
            scratch(5, 6, 32768),
            scratch(4, 64, 128),
            scratch(6, *block),
            scratch(*block),
            scratch(*block),
            scratch(*block),
            scratch(5, 1024, 128),
            scratch(5, 36 * 64, 128),
            scratch(5, 33 * 32, 128),
            scratch(34 * 48, 128),
            scratch(1024, 128),
            scratch(2, 320, 128), scratch(2, 320, 128), scratch(2, 320, 128), scratch(2, 320, 128),
            scratch(2, 32, 128), scratch(2, 32, 128), scratch(2, 32, 128), scratch(2, 32, 128),
            scratch(128, 1024),
            scratch(16, 8, 1024),
            scratch(256, 512),
            scratch(256, 512),
            scratch(256, 512),
            scratch(16, 8, 1024),
            scratch(128, 1024),
            scratch(8, 8, 512),
            scratch(16, 8, 128),
            scratch(8, 8, 128),
            scratch(128, 128), scratch(128, 128), scratch(512, 512), scratch(512, 512),
            scratch(2, 8, 512),
            pltpu.SemaphoreType.DMA((10,)),
            pltpu.SemaphoreType.DMA((N_SEM,)),
            pltpu.SemaphoreType.DMA((N_SEM,)),
        ],
        compiler_params=pltpu.CompilerParams(
            collective_id=0, has_side_effects=True, vmem_limit_bytes=56 * 1024 * 1024
        ),
        name="step",
    )(st, before_start, time_step.reshape(1, 1), *consts)

    where = jnp.stack([lax.axis_index("gx"), lax.axis_index("gy")]).astype(jnp.int32)
    out = pl.pallas_call(
        place_kernel,
        out_shape=jax.ShapeDtypeStruct((5, 6, 32768), f32),
        grid=(5,),
        in_specs=[smem, smem, pl.BlockSpec((6, 1, 32, 8, 128), lambda f: (0, f, 0, 0, 0))],
        out_specs=pl.BlockSpec((1, 6, 32768), lambda f: (f, 0, 0)),
        scratch_shapes=[scratch(4, 64, 128)],
        compiler_params=pltpu.CompilerParams(vmem_limit_bytes=32 * 1024 * 1024),
        name="place",
    )(after_start, where, nb)
    return jnp.transpose(out, (1, 0, 2)), added.reshape(())


def solution(mesh):
    consts = tables()

    def run(*args):
        return per_device([jnp.asarray(c) for c in consts], *args)

    placed = (P(("gx", "gy"), None, None), P(), P(), P())
    return jax.shard_map(
        run,
        mesh=mesh,
        in_specs=placed,
        out_specs=(P(("gx", "gy"), None, None), P()),
        check_vma=False,
    )
```

profile of v0, /device:TPU:1, one launch (start us, length us, event | category | flops | bytes accessed | tf_op | source)
XLA Modules:
  0.0 111.7 jit_solution(160159036311946912)
XLA Ops:
  0.6 0.0 copy-start.1
  1.3 0.1 pad_add_fusion.where
  1.4 101.3 %step.1 = (f32[6,5,32,8,128]{4,3,2,1,0:T(8,128)}, f32[1,1]{1,0:T(1,128)}) custom-call(f32[5,6,32768]{2,1,0:T(8,128)} %bitcast.7, s32[8,16]{1,0:T(8,128)} %before.1, f32[1,1]{1,0:T(1,128)} %bitcast.6.dt_ref, f32[128,128]{1,0:T(8,128)} %constant.19.clone.bz_h, f32[128,128]{1,0:T(8,128)} %constant.20.clone.bzi_h, f32[512,512]{1,0:T(8,128)} %constant.21.clone.sf_h, ...), custom_call_target="tpu_custom_call" | custom-call | tf_op jit(solution)/shard_map/step/pallas_call | solution.py:682
  102.7 0.0 copy-done.1
  102.7 0.0 copy-start
  102.7 2.1 %copy-done = f32[6,5,32,8,128]{4,3,2,1,0:T(8,128)S(1)} copy-done((f32[6,5,32,8,128]{4,3,2,1,0:T(8,128)S(1)}, f32[6,5,32,8,128]{4,3,2,1,0:T(8,128)}, u32[]{:S(2)}) %copy-start) | copy-done | bytes 3932184
  104.8 5.2 %place.1 = f32[5,6,32768]{2,1,0:T(8,128)} custom-call(s32[8,16]{1,0:T(8,128)S(1)} %copy-done.1, s32[2]{0:T(128)S(1)} %pad_add_fusion.where, f32[6,5,32,8,128]{4,3,2,1,0:T(8,128)S(1)} %copy-done), custom_call_target="tpu_custom_call" | custom-call | tf_op jit(solution)/shard_map/place/pallas_call | solution.py:724
Async XLA Ops:
  0.6 102.0 %copy-start.1 = (s32[8,16]{1,0:T(8,128)S(1)}, s32[8,16]{1,0:T(8,128)}, u32[]{:S(2)}) copy-start(s32[8,16]{1,0:T(8,128)} %after.1) | copy-start | bytes 1540
  102.7 2.1 %copy-start = (f32[6,5,32,8,128]{4,3,2,1,0:T(8,128)S(1)}, f32[6,5,32,8,128]{4,3,2,1,0:T(8,128)}, u32[]{:S(2)}) copy-start(f32[6,5,32,8,128]{4,3,2,1,0:T(8,128)} %get-tuple-element.4.nb) | copy-start | bytes 11796484
where the time goes:
time: 114 us; the launch traced here: 112 us
  Pallas kernels  107 us (94%)
  between operations  3.01 us (3%)
  local copies, waits for them, and re-layouts  2.11 us (2%)
    pallas_call x1, Pallas kernels, per_device(): pl.pallas_call(step_kernel, out_shape=(jax.ShapeDtypeStruct((6,) + block,...  101 us
    pallas_call x1, Pallas kernels, per_device(): pl.pallas_call(place_kernel, out_shape=jax.ShapeDtypeStruct((5, 6, 32768)...  5.22 us

commit v1 on v0

v1 whole, which is shorter than its diff:
```python
import jax
import jax.numpy as jnp
import numpy as np
from jax import lax
from jax.experimental import pallas as pl
from jax.experimental.pallas import tpu as pltpu
from jax.sharding import PartitionSpec as P

GAMMA = 5.0 / 3.0
FLOOR = 0.25
MESH = pl.DeviceIdType.MESH
HIGHEST = lax.Precision.HIGHEST

NK, NG, PART = 16, 8, 8
Z_FIRST = 24


def tables():
    def sine(n):
        i = np.arange(1, n + 1)
        return np.sin(np.pi * ((i[:, None] * i[None, :]) % (2 * (n + 1))) / (n + 1))

    sine_y, sine_z = sine(512), sine(64)
    forward = np.zeros((16, 2, 4, 2, 64))
    for u in range(2):
        forward[:, u, :, u, :] = sine_z.reshape(16, 4, 64)
    forward = forward.reshape(128, 128)
    backward = forward * (2.0 / 65)
    padded = np.pad(backward.reshape(128, 2, 64), ((0, 0), (0, 0), (1, 1)))
    slope = (padded[:, :, 2:] - padded[:, :, :-2]).reshape(128, 128)
    order = np.arange(512).reshape(16, 8, 4).transpose(0, 2, 1).reshape(512)
    ordered = sine_y[order]
    modes_y = 2 - 2 * np.cos(np.pi * np.arange(1, 513) / 513)
    modes_z = 2 - 2 * np.cos(np.pi * np.arange(1, 65) / 65)
    h = 0.5 * (modes_z[:, None] + modes_y[None, :])
    root = np.sqrt(h * (h + 2))
    lam = 1 / (1 + h + root)
    gain = -0.5 / root

    def rows(values):
        return np.broadcast_to(values.reshape(16, 1, 4, 512), (16, 2, 4, 512)).reshape(16, 8, 512)

    table = np.stack([rows(lam), rows(gain)], axis=1)
    cell = np.arange(128)
    down = (cell[:, None] == cell - (cell % 64 > 0)).astype(np.float32)
    up = (cell[:, None] == cell + (cell % 64 < 63)).astype(np.float32)
    f32 = np.float32
    return (
        (forward * (4.0 / 64)).astype(f32),
        np.concatenate([backward, slope], axis=1).astype(f32),
        ordered.astype(f32),
        np.ascontiguousarray(ordered.T * (2.0 / 513)).astype(f32),
        table.astype(f32),
        np.tile(np.concatenate([down, up], axis=1), (2, 1)),
    )


def lanes():
    return lax.broadcasted_iota(jnp.int32, (8, 128), 1)


def swap4(parts):
    group = lanes() // 32
    low, even = group < 2, group % 2 == 0

    def pick(order):
        return jnp.where(low, jnp.where(even, order[0], order[1]), jnp.where(even, order[2], order[3]))

    turned = []
    for r in range(4):
        mixed = pick([parts[(i + r) % 4] for i in range(4)])
        turned.append(pltpu.roll(mixed, 32 * r, 1) if r else mixed)
    return [pick([turned[(b - j) % 4] for b in range(4)]) for j in range(4)]


def half_slope(down, up):
    quarter = 0.25 * (down + up)
    low = jnp.minimum(jnp.maximum(down, up), 0.0)
    high = jnp.maximum(jnp.minimum(down, up), 0.0)
    return jnp.minimum(jnp.maximum(quarter, low), high)


def face_flux(left, right, normal):
    def side(w):
        rho, vx, vy, vz, p = w
        gp = GAMMA * p
        return gp * lax.rsqrt(gp * rho), 0.5 * (vx * vx + vy * vy + vz * vz)

    sound_l, half_l = side(left)
    sound_r, half_r = side(right)
    ul, ur = left[1 + normal], right[1 + normal]
    fast = jnp.maximum(jnp.maximum(ul + sound_l, ur + sound_r), 0.0)
    slow = jnp.minimum(jnp.minimum(ul - sound_l, ur - sound_r), 0.0)
    inverse = 1.0 / (fast - slow)
    a, b = fast * inverse, slow * inverse
    d = fast * b
    kl, kr = a * ul - d, d - b * ur
    gl, gr = left[0] * kl, right[0] * kr
    apl, bpr = a * left[4], b * right[4]
    out = [gl + gr]
    for i in range(3):
        term = gl * left[1 + i] + gr * right[1 + i]
        out.append(term + (apl - bpr) if i == normal else term)
    out.append(
        1.5 * (left[4] * kl + right[4] * kr) + (gl * half_l + gr * half_r) + (apl * ul - bpr * ur)
    )
    return out


def cell_flux(w, normal):
    rho, p, u = w[0], w[4], w[1 + normal]
    mass = rho * u
    out = [mass]
    for i in range(3):
        out.append(mass * w[1 + i] + p if i == normal else mass * w[1 + i])
    half = 0.5 * (w[1] * w[1] + w[2] * w[2] + w[3] * w[3])
    out.append(2.5 * p * u + mass * half)
    return out


def at8(row):
    return pl.ds(pl.multiple_of(row, 8), 8)


EDGE, REST, HALO, PHI, AFTER, A2A, BACK, MOM, DEF_Y, DEF_X, N_SEM = (
    0, 2, 8, 12, 16, 24, 40, 56, 64, 80, 88,
)


def step_kernel(
    st, before, dt_ref, bz_h, bzi_h, sf_h, si_h, tab_h, move_h,
    nb, added,
    raw, tmp, dense, tail, next_head, prev_tail, cons, prim, acc, below, above, pot, pot0, potz,
    xs, xr, ys, yr, pxs, pxr, pys, pyr,
    spec_t, spec_r, lines, trans, vsol, back_t, back_r, mom, defs, dgx,
    bz, bzi, sf, si, tab, move, load_sem, ss, rs,
):
    g, k = lax.axis_index("gx"), lax.axis_index("gy")
    k_up, k_dn = (k + 1) % NK, (k + NK - 1) % NK
    g_up, g_dn = (g + 1) % NG, (g + NG - 1) % NG
    dt = dt_ref[0, 0]
    lane = lanes()
    sub = lax.broadcasted_iota(jnp.int32, (8, 128), 0)
    zed = lane % 64

    loads = [pltpu.make_async_copy(st.at[f], raw.at[f], load_sem.at[f]) for f in range(5)]
    consts = [(bz_h, bz), (sf_h, sf), (tab_h.at[k], tab), (si_h, si), (bzi_h, bzi), (move_h, move)]
    const_loads = [
        pltpu.make_async_copy(a, b, load_sem.at[5 + i]) for i, (a, b) in enumerate(consts)
    ]
    for c in loads + const_loads:
        c.start()

    barrier = pltpu.get_barrier_semaphore()

    def greet_y(o, _):
        pl.semaphore_signal(barrier, inc=1, device_id={"gy": (k + o) % NK}, device_id_type=MESH)
        return 0

    def greet_x(o, _):
        pl.semaphore_signal(barrier, inc=1, device_id={"gx": (g + o) % NG}, device_id_type=MESH)
        return 0

    lax.fori_loop(1, NK, greet_y, 0)
    lax.fori_loop(1, NG, greet_x, 0)

    def send(src, dst, sem, device, rsem=None):
        return pltpu.make_async_remote_copy(
            src_ref=src, dst_ref=dst, send_sem=ss.at[sem], recv_sem=rs.at[sem if rsem is None else rsem],
            device_id=device, device_id_type=MESH,
        )

    begin = before[g, k]
    end = jnp.where(k < NK - 1, before[g, jnp.minimum(k + 1, NK - 1)], 4 * NK)
    lead, trail = jnp.clip(begin - 4 * k, -1, 1), jnp.clip(end - 4 * (k + 1), -1, 1)
    last = jnp.clip(end - begin - 1, 0, 5)

    def spread(f):
        def body(x4, _):
            for i4 in range(4):
                x = x4 * 4 + i4
                v = raw[f, :, pl.ds(pl.multiple_of(x * 1024, 1024), 1024)]
                for s in range(8):
                    tmp[i4, 8 * s : 8 * s + 6, :] = v[:, 128 * s : 128 * s + 128]
                for slot in range(6):
                    dense[slot, f, x] = tmp[i4, pl.ds(slot, 8, stride=8), :]
            return 0

        lax.fori_loop(0, 8, body, 0)

        def tails(x4, _):
            for i4 in range(4):
                tail[f, x4 * 4 + i4] = dense[last, f, x4 * 4 + i4]
            return 0

        lax.fori_loop(0, 8, tails, 0)

    def assemble(f):
        def body(x4, _):
            for i4 in range(4):
                x = x4 * 4 + i4
                q0 = jnp.where(lead > 0, prev_tail[f, x], dense[jnp.maximum(-lead, 0), f, x])
                q1 = dense[1 - lead, f, x]
                q2 = dense[2 - lead, f, x]
                q3 = jnp.where(trail < 0, next_head[f, x], dense[3 - lead, f, x])
                for j, v in enumerate(swap4((q0, q2, q1, q3))):
                    cons[f, at8(x * 32 + 8 * j), :] = v
            return 0

        lax.fori_loop(0, 8, body, 0)

    for f in range(5):
        loads[f].wait()
        spread(f)
    pl.semaphore_wait(barrier, NK + NG - 2)
    edges = [
        send(dense.at[0, 0], next_head.at[0], EDGE, {"gy": k_dn}),
        send(tail.at[0], prev_tail.at[0], EDGE + 1, {"gy": k_up}),
    ]
    rest = [
        [
            send(dense.at[0, span], next_head.at[span], REST + 2 * i, {"gy": k_dn}),
            send(tail.at[span], prev_tail.at[span], REST + 2 * i + 1, {"gy": k_up}),
        ]
        for i, span in enumerate((pl.ds(1, 1), pl.ds(2, 1), pl.ds(3, 2)))
    ]
    for c in edges + rest[0]:
        c.start()
    for c in edges:
        c.wait_recv()
    assemble(0)
    for c in const_loads:
        c.wait()

    spec_t[...] = lax.dot_general(
        bz[...], cons[0], (((1,), (1,)), ((), ())),
        precision=HIGHEST, preferred_element_type=jnp.float32,
    )

    def a2a_copy(peer, source):
        return send(
            spec_t.at[at8(8 * peer), :], spec_r.at[source], A2A + peer, {"gy": peer}, A2A + source
        )

    def start_a2a(o, _):
        a2a_copy((k + o) % NK, k).start()
        return 0

    lax.fori_loop(1, NK, start_a2a, 0)
    for c in rest[1]:
        c.start()
    spec_r[k] = spec_t[at8(8 * k), :]
    for c in rest[0]:
        c.wait_recv()
    assemble(1)

    def wait_a2a(o, _):
        source = (k + NK - o) % NK
        a2a_copy(source, source).wait_recv()
        return 0

    lax.fori_loop(1, NK, wait_a2a, 0)

    def to_lines(x4, _):
        for m in range(4):
            parts = [
                spec_r[4 * m + b, :, pl.ds(pl.multiple_of(x4 * 128, 128), 128)] for b in range(4)
            ]
            for i, v in enumerate(swap4(parts)):
                lines[at8(x4 * 32 + 8 * i), 128 * m : 128 * m + 128] = v
        return 0

    lax.fori_loop(0, 8, to_lines, 0)
    trans[...] = jnp.dot(
        lines[...], sf[...], precision=HIGHEST, preferred_element_type=jnp.float32
    )

    lam, gain = tab[0], tab[1]
    lam2 = lam * lam
    lam4 = lam2 * lam2
    lam8 = lam4 * lam4
    lam16 = lam8 * lam8
    lam32 = lam16 * lam16
    lam64 = lam32 * lam32

    def sums(i, carry):
        u, v = carry
        return trans[at8(8 * i), :] + lam * u, trans[at8(8 * (31 - i)), :] + lam * v

    zero = jnp.zeros((8, 512), jnp.float32)
    up_sum, down_sum = lax.fori_loop(0, 32, sums, (zero, zero))
    upper = lax.broadcasted_iota(jnp.int32, (8, 512), 0) >= 4
    up_roll, down_roll = pltpu.roll(up_sum, 4, 0), pltpu.roll(down_sum, 4, 0)
    mom[g] = jnp.where(upper, up_sum + lam32 * up_roll, down_sum + lam32 * down_roll)

    def mom_copy(peer, source):
        return send(mom.at[source], mom.at[source], MOM + peer, {"gx": peer}, MOM + source)

    def start_mom(o, _):
        mom_copy((g + o) % NG, g).start()
        return 0

    lax.fori_loop(1, NG, start_mom, 0)
    for c in rest[2]:
        c.start()

    def wait_mom(o, _):
        source = (g + NG - o) % NG
        mom_copy(source, source).wait_recv()
        return 0

    lax.fori_loop(1, NG, wait_mom, 0)
    from_low, from_high, at_start, at_end = zero, zero, zero, zero
    power_low, power_high = zero + 1.0, zero + 1.0
    for i in range(NG):
        m_up, m_dn = mom[i], mom[NG - 1 - i]
        ups = jnp.where(upper, m_up, pltpu.roll(m_up, 4, 0))
        downs = jnp.where(upper, pltpu.roll(m_dn, 4, 0), m_dn)
        from_low = jnp.where(i < g, from_low * lam64 + ups, from_low)
        from_high = jnp.where(NG - 1 - i > g, from_high * lam64 + downs, from_high)
        at_end = at_end * lam64 + ups
        at_start = at_start * lam64 + downs
        power_low = jnp.where(i < g, power_low * lam64, power_low)
        power_high = jnp.where(NG - 1 - i > g, power_high * lam64, power_high)
    lam128 = lam64 * lam64
    lam256 = lam128 * lam128
    whole = lam256 * lam256 * lam
    at_start, at_end = lam * at_start, lam * at_end
    scale = 1.0 / (1.0 - whole * whole)
    from_low = from_low - (at_start - whole * at_end) * scale * power_low
    from_high = from_high - (at_end - whole * at_start) * scale * power_high
    first_u = jnp.where(upper, up_roll + lam32 * from_low, from_low)
    first_v = jnp.where(upper, from_high, down_roll + lam32 * from_high)

    def downward(i, v):
        v = trans[at8(8 * (31 - i)), :] + lam * v
        vsol[at8(8 * (31 - i)), :] = v
        return v

    lax.fori_loop(0, 32, downward, first_v)

    def upward(i, u):
        carried = lam * u
        f = trans[at8(8 * i), :]
        trans[at8(8 * i), :] = gain * (carried + vsol[at8(8 * i), :])
        return f + carried

    lax.fori_loop(0, 32, upward, first_u)
    lines[...] = jnp.dot(
        trans[...], si[...], precision=HIGHEST, preferred_element_type=jnp.float32
    )

    def from_lines(x4, _):
        for m in range(4):
            parts = [lines[at8(x4 * 32 + 8 * i), 128 * m : 128 * m + 128] for i in range(4)]
            for b, v in enumerate(swap4(parts)):
                back_t[4 * m + b, :, pl.ds(pl.multiple_of(x4 * 128, 128), 128)] = v
        return 0

    lax.fori_loop(0, 8, from_lines, 0)

    def back_copy(peer, source):
        return send(
            back_t.at[peer], back_r.at[at8(8 * source), :], BACK + peer, {"gy": peer}, BACK + source
        )

    def start_back(o, _):
        back_copy((k + o) % NK, k).start()
        return 0

    lax.fori_loop(1, NK, start_back, 0)
    back_r[at8(8 * k), :] = back_t[k]

    for c in rest[1] + rest[2]:
        c.wait_recv()
    for f in range(2, 5):
        assemble(f)

    def primitives(x, _):
        for j in range(4):
            rho, mx, my, mz, energy = [cons[f, at8(x * 32 + 8 * j), :] for f in range(5)]
            inverse = 1.0 / rho
            vx, vy, vz = mx * inverse, my * inverse, mz * inverse
            p = (GAMMA - 1.0) * (energy - 0.5 * rho * (vx * vx + vy * vy + vz * vz))
            for f, v in enumerate((rho, vx, vy, vz, p)):
                prim[f, at8((x + 2) * 64 + (j + 2) * 8), :] = v
        return 0

    lax.fori_loop(0, 32, primitives, 0)

    for f in range(5):
        for r in range(2):
            for j in range(4):
                row = f * 64 + r * 32 + j * 8
                xs[0, row : row + 8, :] = prim[f, (2 + r) * 64 + (j + 2) * 8 : (2 + r) * 64 + (j + 3) * 8, :]
                xs[1, row : row + 8, :] = prim[f, (32 + r) * 64 + (j + 2) * 8 : (32 + r) * 64 + (j + 3) * 8, :]
            for q in range(4):
                row = f * 64 + r * 32 + q * 8
                ys[0, row : row + 8, :] = prim[f, pl.ds((2 + 8 * q) * 64 + (2 + r) * 8, 8, stride=64), :]
                ys[1, row : row + 8, :] = prim[f, pl.ds((2 + 8 * q) * 64 + (4 + r) * 8 + 7, 8, stride=64), :]
    halo = [
        send(xs.at[0], xr.at[1], HALO, {"gx": g_dn}),
        send(xs.at[1], xr.at[0], HALO + 1, {"gx": g_up}),
        send(ys.at[0], yr.at[1], HALO + 2, {"gy": k_dn}),
        send(ys.at[1], yr.at[0], HALO + 3, {"gy": k_up}),
    ]
    for c in halo:
        c.start()

    def neighbours_z(x8, _):
        for f in range(5):
            v = jnp.concatenate(
                [prim[f, pl.ds(pl.multiple_of((x8 * 8 + i + 2) * 64 + 16, 16), 32), :] for i in range(8)]
            )
            upper_half = v.astype(jnp.bfloat16)
            lower_half = (v - upper_half.astype(jnp.float32)).astype(jnp.bfloat16)
            both = jnp.dot(
                jnp.concatenate([upper_half, lower_half], axis=1), move[...],
                preferred_element_type=jnp.float32,
            )
            rows = pl.ds(pl.multiple_of(x8 * 256, 256), 256)
            below[f, rows, :] = both[:, 0:128]
            above[f, rows, :] = both[:, 128:256]
        return 0

    lax.fori_loop(0, 4, neighbours_z, 0)

    def sweep_z(x, _):
        for j in range(4):
            row = at8(x * 32 + 8 * j)
            w = [prim[f, at8((x + 2) * 64 + (j + 2) * 8), :] for f in range(5)]
            left, right = [], []
            for f, v in enumerate(w):
                h = half_slope(v - below[f, row, :], above[f, row, :] - v)
                left.append(v + h)
                lower = v - h
                right.append(jnp.where(zed == 63, lower, pltpu.roll(lower, 127, 1)))
            high = face_flux(left, right, 2)
            wall = cell_flux(w, 2)
            for f in range(5):
                low = jnp.where(zed == 0, wall[f], pltpu.roll(high[f], 1, 1))
                acc[f, row, :] = high[f] - low
        return 0

    lax.fori_loop(0, Z_FIRST, sweep_z, 0)

    def wait_back(o, _):
        source = (k + NK - o) % NK
        back_copy(source, source).wait_recv()
        return 0

    lax.fori_loop(1, NK, wait_back, 0)
    both = lax.dot_general(
        back_r[...], bzi[...], (((0,), (0,)), ((), ())),
        precision=HIGHEST, preferred_element_type=jnp.float32,
    )
    pot0[...] = both[:, 0:128]
    potz[...] = both[:, 128:256]
    pxs[0] = pot0[0:32, :]
    pxs[1] = pot0[31 * 32 : 32 * 32, :]
    for q in range(4):
        pys[0, 8 * q : 8 * q + 8, :] = pot0[pl.ds(8 * q * 32, 8, stride=32), :]
        pys[1, 8 * q : 8 * q + 8, :] = pot0[pl.ds(8 * q * 32 + 31, 8, stride=32), :]
    phi_halo = [
        send(pxs.at[0], pxr.at[1], PHI, {"gx": g_dn}),
        send(pxs.at[1], pxr.at[0], PHI + 1, {"gx": g_up}),
        send(pys.at[0], pyr.at[1], PHI + 2, {"gy": k_dn}),
        send(pys.at[1], pyr.at[0], PHI + 3, {"gy": k_up}),
    ]
    for c in phi_halo:
        c.start()

    lax.fori_loop(Z_FIRST, 32, sweep_z, 0)

    for c in halo:
        c.wait_recv()

    for f in range(5):
        for r in range(2):
            for j in range(4):
                row = f * 64 + r * 32 + j * 8
                e = (j + 2) * 8

                def plane(xx):
                    return prim[f, (xx + 2) * 64 + e : (xx + 2) * 64 + e + 8, :]

                low = pltpu.roll(jnp.where(lane >= 64, xr[0, row : row + 8, :], plane(30 + r)), 64, 1)
                low = jnp.where((lane < 64) & (g == 0), plane(0), low)
                prim[f, r * 64 + e : r * 64 + e + 8, :] = low
                high = pltpu.roll(jnp.where(lane < 64, xr[1, row : row + 8, :], plane(r)), 64, 1)
                high = jnp.where((lane >= 64) & (g == NG - 1), plane(31), high)
                prim[f, (34 + r) * 64 + e : (34 + r) * 64 + e + 8, :] = high

    def place_y(x, _):
        base = (x + 2) * 64
        for f in range(5):
            rows = [prim[f, at8(base + 16 + 8 * j), :] for j in range(4)]
            first = jnp.broadcast_to(rows[0][0:1, :], (8, 128))
            final = jnp.broadcast_to(rows[3][7:8, :], (8, 128))
            for r in range(2):
                row = f * 64 + r * 32 + x
                low = jnp.where(k == 0, first, jnp.broadcast_to(yr[0, pl.ds(row, 1), :], (8, 128)))
                prim[f, at8(base + 8 * r), :] = jnp.where(sub == 0, low, pltpu.roll(rows[2 + r], 1, 0))
                high = jnp.where(k == NK - 1, final, jnp.broadcast_to(yr[1, pl.ds(row, 1), :], (8, 128)))
                prim[f, at8(base + 48 + 8 * r), :] = jnp.where(sub == 7, high, pltpu.roll(rows[r], 7, 0))
        return 0

    lax.fori_loop(0, 32, place_y, 0)

    def sweep_row(cell, count, normal, target):
        before_left, before_flux = None, None
        for i in range(-1, count + 1):
            left, right = [], []
            for f in range(5):
                v = cell(f, i)
                h = half_slope(v - cell(f, i - 1), cell(f, i + 1) - v)
                left.append(v + h)
                right.append(v - h)
            if before_left is not None:
                flux = face_flux(before_left, right, normal)
                if before_flux is not None:
                    for f in range(5):
                        row = target(i - 1)
                        acc[f, row, :] = acc[f, row, :] + (flux[f] - before_flux[f])
                before_flux = flux
            before_left = left

    def hydro(part):
        def sweep_y(i, _):
            x = part * PART + i
            base = (x + 2) * 64 + 16
            sweep_row(
                lambda f, e: prim[f, at8(base + 8 * e), :], 4, 1, lambda e: at8(x * 32 + 8 * e)
            )
            return 0

        lax.fori_loop(0, PART, sweep_y, 0)

        def sweep_x(j, _):
            base = (part * PART + 2) * 64 + 16 + 8 * j
            sweep_row(
                lambda f, i: prim[f, at8(base + 64 * i), :], PART, 0,
                lambda i: at8((part * PART + i) * 32 + 8 * j),
            )
            return 0

        lax.fori_loop(0, 4, sweep_x, 0)

    def finish(part):
        def body(i, _):
            x = part * PART + i
            base = (x + 1) * 48 + 8
            new = [[None] * 4 for _ in range(5)]
            half = -0.5 * dt
            for j in range(4):
                ax = half * (pot[at8(base + 48 + 8 * j), :] - pot[at8(base - 48 + 8 * j), :])
                ay = half * (pot[at8(base + 8 + 8 * j), :] - pot[at8(base - 8 + 8 * j), :])
                az = half * potz[at8(x * 32 + 8 * j), :]
                u = [cons[f, at8(x * 32 + 8 * j), :] for f in range(5)]
                change = [acc[f, at8(x * 32 + 8 * j), :] for f in range(5)]
                new[0][j] = jnp.maximum(u[0] - dt * change[0], FLOOR)
                for i3, a in enumerate((ax, ay, az)):
                    new[1 + i3][j] = u[1 + i3] - dt * change[1 + i3] + u[0] * a
                new[4][j] = u[4] - dt * change[4] + (u[1] * ax + u[2] * ay + u[3] * az)
            for f in range(5):
                b0, b2, b1, b3 = swap4(new[f])
                for q, v in enumerate((b0, b1, b2, b3)):
                    nb[1 + q, f, x] = v
            return 0

        lax.fori_loop(0, PART, body, 0)

    def after_copies(part):
        span = pl.ds(part * PART, PART)
        return [
            send(nb.at[1, :, span], nb.at[5, :, span], AFTER + part, {"gy": k_dn}),
            send(nb.at[4, :, span], nb.at[0, :, span], AFTER + 4 + part, {"gy": k_up}),
        ]

    def emit(part):
        for c in after_copies(part):
            c.start()

    def hydro_part(part, _):
        hydro(part)
        return 0

    lax.fori_loop(0, 32 // PART, hydro_part, 0)

    def deficit(x, total):
        for j in range(4):
            row = at8(x * 32 + 8 * j)
            density = cons[0, row, :] - dt * acc[0, row, :]
            total = total + (jnp.maximum(density, FLOOR) - density)
        return total

    defs[k] = lax.fori_loop(0, 32, deficit, jnp.zeros((8, 128), jnp.float32))

    def def_copy(peer, source):
        return send(defs.at[source], defs.at[source], DEF_Y + peer, {"gy": peer}, DEF_Y + source)

    def start_def(o, _):
        def_copy((k + o) % NK, k).start()
        return 0

    def wait_def(o, _):
        source = (k + NK - o) % NK
        def_copy(source, source).wait_recv()
        return 0

    lax.fori_loop(1, NK, start_def, 0)

    for c in phi_halo:
        c.wait_recv()
    for j in range(4):
        low = pltpu.roll(
            jnp.where(lane >= 64, pxr[0, 8 * j : 8 * j + 8, :], pot0[31 * 32 + 8 * j : 31 * 32 + 8 * j + 8, :]), 64, 1
        )
        pot[8 + 8 * j : 16 + 8 * j, :] = jnp.where((lane < 64) & (g == 0), 0.0, low)
        high = pltpu.roll(jnp.where(lane < 64, pxr[1, 8 * j : 8 * j + 8, :], pot0[8 * j : 8 * j + 8, :]), 64, 1)
        pot[33 * 48 + 8 + 8 * j : 33 * 48 + 16 + 8 * j, :] = jnp.where((lane >= 64) & (g == NG - 1), 0.0, high)

    def place_pot(x, _):
        base = (x + 1) * 48
        rows = [pot0[at8(x * 32 + 8 * j), :] for j in range(4)]
        for j in range(4):
            pot[at8(base + 8 + 8 * j), :] = rows[j]
        low = jnp.where(k == 0, 0.0, jnp.broadcast_to(pyr[0, pl.ds(x, 1), :], (8, 128)))
        pot[at8(base), :] = jnp.where(sub == 0, low, pltpu.roll(rows[3], 1, 0))
        high = jnp.where(k == NK - 1, 0.0, jnp.broadcast_to(pyr[1, pl.ds(x, 1), :], (8, 128)))
        pot[at8(base + 40), :] = jnp.where(sub == 7, high, pltpu.roll(rows[0], 7, 0))
        return 0

    lax.fori_loop(0, 32, place_pot, 0)
    def one_part(part, _):
        finish(part)
        emit(part)
        return 0

    lax.fori_loop(0, 2, one_part, 0)
    lax.fori_loop(1, NK, wait_def, 0)
    dgx[g] = jnp.sum(defs[...], axis=0)

    def dgx_copy(peer, source):
        return send(dgx.at[source], dgx.at[source], DEF_X + peer, {"gx": peer}, DEF_X + source)

    def start_dgx(o, _):
        dgx_copy((g + o) % NG, g).start()
        return 0

    def wait_dgx(o, _):
        source = (g + NG - o) % NG
        dgx_copy(source, source).wait_recv()
        return 0

    lax.fori_loop(1, NG, start_dgx, 0)
    lax.fori_loop(2, 4, one_part, 0)
    lax.fori_loop(1, NG, wait_dgx, 0)
    added[0, 0] = jnp.sum(jnp.sum(dgx[...], axis=0)) * (1.0 / 512)

    for c in edges + rest[0] + rest[1] + rest[2] + halo + phi_halo:
        c.wait_send()

    def sent_y(o, _):
        peer = (k + o) % NK
        a2a_copy(peer, k).wait_send()
        back_copy(peer, k).wait_send()
        def_copy(peer, k).wait_send()
        return 0

    def sent_x(o, _):
        peer = (g + o) % NG
        mom_copy(peer, g).wait_send()
        dgx_copy(peer, g).wait_send()
        return 0

    lax.fori_loop(1, NK, sent_y, 0)
    lax.fori_loop(1, NG, sent_x, 0)
    for part in range(32 // PART):
        for c in after_copies(part):
            c.wait()


def place_kernel(after, where, nb, out, tmp, ready, sem):
    g, k = where[0], where[1]
    begin = after[g, k]
    end = jnp.where(k < NK - 1, after[g, jnp.minimum(k + 1, NK - 1)], 4 * NK)
    lead, held = jnp.clip(begin - 4 * k, -1, 1), end - begin
    writes = [pltpu.make_async_copy(ready.at[f], out.at[f], sem.at[f]) for f in range(5)]
    for f in range(5):

        def body(x4, _):
            for i4 in range(4):
                x = x4 * 4 + i4
                for slot in range(6):
                    index = jnp.minimum(slot + lead + 1, 5)
                    v = jnp.where(slot < held, nb[index, f, x], 0.0)
                    tmp[i4, pl.ds(slot, 8, stride=8), :] = v
                for s in range(8):
                    ready[f, :, pl.ds(pl.multiple_of(x * 1024 + 128 * s, 128), 128)] = tmp[i4, 8 * s : 8 * s + 6, :]
            return 0

        lax.fori_loop(0, 8, body, 0)
        writes[f].start()
    for c in writes:
        c.wait()


def per_device(consts, state_before, before_start, after_start, time_step):
    f32 = jnp.float32
    st = jnp.transpose(state_before, (1, 0, 2))
    any_spec = pl.BlockSpec(memory_space=pl.ANY)
    smem = pl.BlockSpec(memory_space=pltpu.SMEM)
    vmem = pl.BlockSpec(memory_space=pltpu.VMEM)
    block = (5, 32, 8, 128)

    def scratch(*shape):
        return pltpu.VMEM(shape, f32)

    nb, added = pl.pallas_call(
        step_kernel,
        out_shape=(pltpu.VMEM((6,) + block, f32), jax.ShapeDtypeStruct((1, 1), f32)),
        in_specs=[any_spec, smem, smem] + [any_spec] * 6,
        out_specs=(vmem, smem),
        scratch_shapes=[
            scratch(5, 6, 32768),
            scratch(4, 64, 128),
            scratch(6, *block),
            scratch(*block),
            scratch(*block),
            scratch(*block),
            scratch(5, 1024, 128),
            scratch(5, 36 * 64, 128),
            scratch(5, 1024, 128),
            scratch(5, 1024, 128), scratch(5, 1024, 128),
            scratch(34 * 48, 128),
            scratch(1024, 128),
            scratch(1024, 128),
            scratch(2, 320, 128), scratch(2, 320, 128), scratch(2, 320, 128), scratch(2, 320, 128),
            scratch(2, 32, 128), scratch(2, 32, 128), scratch(2, 32, 128), scratch(2, 32, 128),
            scratch(128, 1024),
            scratch(16, 8, 1024),
            scratch(256, 512),
            scratch(256, 512),
            scratch(256, 512),
            scratch(16, 8, 1024),
            scratch(128, 1024),
            scratch(8, 8, 512),
            scratch(16, 8, 128),
            scratch(8, 8, 128),
            scratch(128, 128), scratch(128, 256), scratch(512, 512), scratch(512, 512),
            scratch(2, 8, 512),
            pltpu.VMEM((256, 256), jnp.bfloat16),
            pltpu.SemaphoreType.DMA((11,)),
            pltpu.SemaphoreType.DMA((N_SEM,)),
            pltpu.SemaphoreType.DMA((N_SEM,)),
        ],
        compiler_params=pltpu.CompilerParams(
            collective_id=0, has_side_effects=True, vmem_limit_bytes=58 * 1024 * 1024
        ),
        name="step",
    )(st, before_start, time_step.reshape(1, 1), *consts)

    where = jnp.stack([lax.axis_index("gx"), lax.axis_index("gy")]).astype(jnp.int32)
    out = pl.pallas_call(
        place_kernel,
        out_shape=jax.ShapeDtypeStruct((5, 6, 32768), f32),
        in_specs=[smem, smem, vmem],
        out_specs=any_spec,
        scratch_shapes=[
            scratch(4, 64, 128), scratch(5, 6, 32768), pltpu.SemaphoreType.DMA((5,)),
        ],
        compiler_params=pltpu.CompilerParams(vmem_limit_bytes=32 * 1024 * 1024),
        name="place",
    )(after_start, where, nb)
    return jnp.transpose(out, (1, 0, 2)), added.reshape(())


def solution(mesh):
    consts = tables()

    def run(*args):
        return per_device([jnp.asarray(c) for c in consts[:-1]] + [jnp.asarray(consts[-1], jnp.bfloat16)], *args)

    placed = (P(("gx", "gy"), None, None), P(), P(), P())
    return jax.shard_map(
        run,
        mesh=mesh,
        in_specs=placed,
        out_specs=(P(("gx", "gy"), None, None), P()),
        check_vma=False,
    )
```

time: 114 us -> 86.9 us (0.76)
  the two profiles are of different devices: /device:TPU:1 before, /device:TPU:8 now
where the time goes in v1:
time: 86.9 us; the launch traced here: 86.7 us
  Pallas kernels  83.6 us (96%)
  between operations  3.08 us (4%)
    pallas_call x1, Pallas kernels, per_device(): pl.pallas_call(step_kernel, out_shape=(pltpu.VMEM((6,) + block, f32), jax...  79.8 us
    pallas_call x1, Pallas kernels, per_device(): pl.pallas_call(place_kernel, out_shape=jax.ShapeDtypeStruct((5, 6, 32768)...  3.83 us

profile of v1, /device:TPU:8, one launch (start us, length us, event | category | flops | bytes accessed | tf_op | source)
XLA Modules:
  0.0 86.7 jit_solution(12843041696437108112)
XLA Ops:
  0.6 0.0 copy-start
  1.3 0.1 pad_add_fusion.where
  1.4 79.8 %step.1 = (f32[6,5,32,8,128]{4,3,2,1,0:T(8,128)S(1)}, f32[1,1]{1,0:T(1,128)}) custom-call(f32[5,6,32768]{2,1,0:T(8,128)} %bitcast.7, s32[8,16]{1,0:T(8,128)} %before.1, f32[1,1]{1,0:T(1,128)} %bitcast.6.dt_ref, f32[128,128]{1,0:T(8,128)} %constant.21.clone.bz_h, f32[128,256]{1,0:T(8,128)} %constant.22.clone.bzi_h, f32[512,512]{1,0:T(8,128)} %constant.23.clone.sf_h, ...), custom_call_target="tpu_custom_call" | custom-call | tf_op jit(solution)/shard_map/step/pallas_call | solution.py:720
  81.1 0.0 copy-done
  81.2 3.8 %place.1 = f32[5,6,32768]{2,1,0:T(8,128)} custom-call(s32[8,16]{1,0:T(8,128)S(1)} %copy-done, s32[2]{0:T(128)S(1)} %pad_add_fusion.where, f32[6,5,32,8,128]{4,3,2,1,0:T(8,128)S(1)} %get-tuple-element.4.nb), custom_call_target="tpu_custom_call" | custom-call | tf_op jit(solution)/shard_map/place/pallas_call | solution.py:765
Async XLA Ops:
  0.6 80.5 %copy-start = (s32[8,16]{1,0:T(8,128)S(1)}, s32[8,16]{1,0:T(8,128)}, u32[]{:S(2)}) copy-start(s32[8,16]{1,0:T(8,128)} %after.1) | copy-start | bytes 1540

commit v2 on v1

v2 whole, which is shorter than its diff:
```python
import jax
import jax.numpy as jnp
import numpy as np
from jax import lax
from jax.experimental import pallas as pl
from jax.experimental.pallas import tpu as pltpu
from jax.sharding import PartitionSpec as P

GAMMA = 5.0 / 3.0
FLOOR = 0.25
MESH = pl.DeviceIdType.MESH
HIGHEST = lax.Precision.HIGHEST

NK, NG, PART = 16, 8, 8


def tables():
    def sine(n):
        i = np.arange(1, n + 1)
        return np.sin(np.pi * ((i[:, None] * i[None, :]) % (2 * (n + 1))) / (n + 1))

    sine_x, sine_z = sine(512), sine(64)
    forward = np.zeros((8, 2, 8, 2, 64))
    for u in range(2):
        forward[:, u, :, u, :] = sine_z.reshape(8, 8, 64)
    forward = forward.reshape(128, 128)
    backward = forward * (2.0 / 65)
    padded = np.pad(backward.reshape(128, 2, 64), ((0, 0), (0, 0), (1, 1)))
    slope = (padded[:, :, 2:] - padded[:, :, :-2]).reshape(128, 128)
    order = np.arange(512).reshape(8, 2, 8, 4).transpose(0, 1, 3, 2).reshape(512)
    ordered = sine_x[order]
    modes_x = 2 - 2 * np.cos(np.pi * np.arange(1, 513) / 513)
    modes_z = 2 - 2 * np.cos(np.pi * np.arange(1, 65) / 65)
    h = 0.5 * (modes_z[:, None] + modes_x[None, :])
    root = np.sqrt(h * (h + 2))
    lam = 1 / (1 + h + root)
    gain = -0.5 / root

    table = np.stack([lam.reshape(8, 8, 512), gain.reshape(8, 8, 512)], axis=1)
    cell = np.arange(128)
    down = (cell[:, None] == cell - (cell % 64 > 0)).astype(np.float32)
    up = (cell[:, None] == cell + (cell % 64 < 63)).astype(np.float32)
    f32 = np.float32
    return (
        (forward * (4.0 / 64)).astype(f32),
        np.concatenate([backward, slope], axis=1).astype(f32),
        ordered.astype(f32),
        (ordered * (2.0 / 513)).astype(f32),
        table.astype(f32),
        np.tile(np.concatenate([down, up], axis=1), (2, 1)),
    )


def lanes():
    return lax.broadcasted_iota(jnp.int32, (8, 128), 1)


def swap4(parts):
    group = lanes() // 32
    low, even = group < 2, group % 2 == 0

    def pick(order):
        return jnp.where(low, jnp.where(even, order[0], order[1]), jnp.where(even, order[2], order[3]))

    turned = []
    for r in range(4):
        mixed = pick([parts[(i + r) % 4] for i in range(4)])
        turned.append(pltpu.roll(mixed, 32 * r, 1) if r else mixed)
    return [pick([turned[(b - j) % 4] for b in range(4)]) for j in range(4)]


def half_slope(down, up):
    quarter = 0.25 * (down + up)
    low = jnp.minimum(jnp.maximum(down, up), 0.0)
    high = jnp.maximum(jnp.minimum(down, up), 0.0)
    return jnp.minimum(jnp.maximum(quarter, low), high)


def face_flux(left, right, normal):
    def side(w):
        rho, vx, vy, vz, p = w
        gp = GAMMA * p
        return gp * lax.rsqrt(gp * rho), 0.5 * (vx * vx + vy * vy + vz * vz)

    sound_l, half_l = side(left)
    sound_r, half_r = side(right)
    ul, ur = left[1 + normal], right[1 + normal]
    fast = jnp.maximum(jnp.maximum(ul + sound_l, ur + sound_r), 0.0)
    slow = jnp.minimum(jnp.minimum(ul - sound_l, ur - sound_r), 0.0)
    inverse = 1.0 / (fast - slow)
    a, b = fast * inverse, slow * inverse
    d = fast * b
    kl, kr = a * ul - d, d - b * ur
    gl, gr = left[0] * kl, right[0] * kr
    apl, bpr = a * left[4], b * right[4]
    out = [gl + gr]
    for i in range(3):
        term = gl * left[1 + i] + gr * right[1 + i]
        out.append(term + (apl - bpr) if i == normal else term)
    out.append(
        1.5 * (left[4] * kl + right[4] * kr) + (gl * half_l + gr * half_r) + (apl * ul - bpr * ur)
    )
    return out


def cell_flux(w, normal):
    rho, p, u = w[0], w[4], w[1 + normal]
    mass = rho * u
    out = [mass]
    for i in range(3):
        out.append(mass * w[1 + i] + p if i == normal else mass * w[1 + i])
    half = 0.5 * (w[1] * w[1] + w[2] * w[2] + w[3] * w[3])
    out.append(2.5 * p * u + mass * half)
    return out


def at8(row):
    return pl.ds(pl.multiple_of(row, 8), 8)


EDGE, REST, HALO, PHI, AFTER, A2A, BACK, MOM_Z, MOM_Y, DEF_Y, DEF_X, DENSITY, N_SEM = (
    0, 2, 10, 20, 24, 32, 40, 48, 52, 56, 72, 80, 88,
)


def step_kernel(
    st, before, dt_ref, bz_h, bzi_h, sf_h, si_h, tab_h, move_h,
    nb, added,
    raw, tmp, dense, tail, next_head, prev_tail, cons, prim, acc, below, above, pot, pot0, potz,
    xs, xr, ys, yr, pxs, pxr, pys, pyr,
    spec_t, spec_r, lines, trans, held, vsol, back_t, back_r, mom_z, mom_y, defs, dgx,
    bz, bzi, sf, si, tab, move, load_sem, ss, rs,
):
    g, k = lax.axis_index("gx"), lax.axis_index("gy")
    k_up, k_dn = (k + 1) % NK, (k + NK - 1) % NK
    g_up, g_dn = (g + 1) % NG, (g + NG - 1) % NG
    dt = dt_ref[0, 0]
    lane = lanes()
    sub = lax.broadcasted_iota(jnp.int32, (8, 128), 0)
    zed = lane % 64

    loads = [pltpu.make_async_copy(st.at[f], raw.at[f], load_sem.at[f]) for f in range(5)]
    consts = [(bz_h, bz), (sf_h, sf), (tab_h.at[g], tab), (si_h, si), (bzi_h, bzi), (move_h, move)]
    const_loads = [
        pltpu.make_async_copy(a, b, load_sem.at[5 + i]) for i, (a, b) in enumerate(consts)
    ]
    for c in loads + const_loads:
        c.start()

    barrier = pltpu.get_barrier_semaphore()

    def greet_y(o, _):
        pl.semaphore_signal(barrier, inc=1, device_id={"gy": (k + o) % NK}, device_id_type=MESH)
        return 0

    def greet_x(o, _):
        pl.semaphore_signal(barrier, inc=1, device_id={"gx": (g + o) % NG}, device_id_type=MESH)
        return 0

    lax.fori_loop(1, NK, greet_y, 0)
    lax.fori_loop(1, NG, greet_x, 0)

    def send(src, dst, sem, device, rsem=None):
        return pltpu.make_async_remote_copy(
            src_ref=src, dst_ref=dst, send_sem=ss.at[sem], recv_sem=rs.at[sem if rsem is None else rsem],
            device_id=device, device_id_type=MESH,
        )

    begin = before[g, k]
    end = jnp.where(k < NK - 1, before[g, jnp.minimum(k + 1, NK - 1)], 4 * NK)
    lead, trail = jnp.clip(begin - 4 * k, -1, 1), jnp.clip(end - 4 * (k + 1), -1, 1)
    last = jnp.clip(end - begin - 1, 0, 5)

    def spread(f):
        def body(x4, _):
            for i4 in range(4):
                x = x4 * 4 + i4
                v = raw[f, :, pl.ds(pl.multiple_of(x * 1024, 1024), 1024)]
                for s in range(8):
                    tmp[i4, 8 * s : 8 * s + 6, :] = v[:, 128 * s : 128 * s + 128]
                for slot in range(6):
                    dense[slot, f, x] = tmp[i4, pl.ds(slot, 8, stride=8), :]
            return 0

        lax.fori_loop(0, 8, body, 0)

        def tails(x4, _):
            for i4 in range(4):
                tail[f, x4 * 4 + i4] = dense[last, f, x4 * 4 + i4]
            return 0

        lax.fori_loop(0, 8, tails, 0)

    def assemble(fields, first, count, step):
        def body(i, _):
            for f in fields:
                for i4 in range(step):
                    x = first + i * step + i4
                    q0 = jnp.where(lead > 0, prev_tail[f, x], dense[jnp.maximum(-lead, 0), f, x])
                    q1 = dense[1 - lead, f, x]
                    q2 = dense[2 - lead, f, x]
                    q3 = jnp.where(trail < 0, next_head[f, x], dense[3 - lead, f, x])
                    for j, v in enumerate(swap4((q0, q2, q1, q3))):
                        cons[f, at8(x * 32 + 8 * j), :] = v
            return 0

        lax.fori_loop(0, count // step, body, 0)

    loads[0].wait()
    spread(0)
    pl.semaphore_wait(barrier, NK + NG - 2)
    edges = [
        send(dense.at[0, 0], next_head.at[0], EDGE, {"gy": k_dn}),
        send(tail.at[0], prev_tail.at[0], EDGE + 1, {"gy": k_up}),
    ]
    rest = [
        [
            send(dense.at[0, pl.ds(1, 4), span], next_head.at[pl.ds(1, 4), span], REST + 2 * i, {"gy": k_dn}),
            send(tail.at[pl.ds(1, 4), span], prev_tail.at[pl.ds(1, 4), span], REST + 2 * i + 1, {"gy": k_up}),
        ]
        for i, span in enumerate(pl.ds(PART * i, PART) for i in range(32 // PART))
    ]
    for c in edges:
        c.start()
    for f in range(1, 5):
        loads[f].wait()
        spread(f)
    for c in rest[0]:
        c.start()
    for c in edges:
        c.wait_recv()
    assemble((0,), 0, 32, 4)
    for c in const_loads:
        c.wait()

    def primitives(x, _):
        for j in range(4):
            rho, mx, my, mz, energy = [cons[f, at8(x * 32 + 8 * j), :] for f in range(5)]
            inverse = 1.0 / rho
            vx, vy, vz = mx * inverse, my * inverse, mz * inverse
            p = (GAMMA - 1.0) * (energy - 0.5 * rho * (vx * vx + vy * vy + vz * vz))
            for f, v in enumerate((rho, vx, vy, vz, p)):
                prim[f, at8((x + 2) * 64 + (j + 2) * 8), :] = v
        return 0

    def neighbours_z(x8, _):
        for f in range(5):
            v = jnp.concatenate(
                [prim[f, pl.ds(pl.multiple_of((x8 * 8 + i + 2) * 64 + 16, 16), 32), :] for i in range(8)]
            )
            upper_half = v.astype(jnp.bfloat16)
            lower_half = (v - upper_half.astype(jnp.float32)).astype(jnp.bfloat16)
            both = jnp.dot(
                jnp.concatenate([upper_half, lower_half], axis=1), move[...],
                preferred_element_type=jnp.float32,
            )
            rows = pl.ds(pl.multiple_of(x8 * 256, 256), 256)
            below[f, rows, :] = both[:, 0:128]
            above[f, rows, :] = both[:, 128:256]
        return 0

    def sweep_z(x, _):
        for j in range(4):
            row = at8(x * 32 + 8 * j)
            w = [prim[f, at8((x + 2) * 64 + (j + 2) * 8), :] for f in range(5)]
            left, right = [], []
            for f, v in enumerate(w):
                h = half_slope(v - below[f, row, :], above[f, row, :] - v)
                left.append(v + h)
                lower = v - h
                right.append(jnp.where(zed == 63, lower, pltpu.roll(lower, 127, 1)))
            high = face_flux(left, right, 2)
            wall = cell_flux(w, 2)
            for f in range(5):
                low = jnp.where(zed == 0, wall[f], pltpu.roll(high[f], 1, 1))
                acc[f, row, :] = high[f] - low
        return 0

    def halo_y(part):
        span = pl.ds(80 * part, 80)
        return [
            send(ys.at[0, span], yr.at[1, span], HALO + 2 * part, {"gy": k_dn}),
            send(ys.at[1, span], yr.at[0, span], HALO + 2 * part + 1, {"gy": k_up}),
        ]

    halo_x = [
        send(xs.at[0], xr.at[1], HALO + 8, {"gx": g_dn}),
        send(xs.at[1], xr.at[0], HALO + 9, {"gx": g_up}),
    ]

    def halo_copies(part):
        return halo_y(part) + (halo_x[:1] if part == 0 else halo_x[1:] if part == 3 else [])

    def send_halo(part):
        for f in range(5):
            for r in range(2):
                row = part * 80 + f * 16 + r * 8
                base = (2 + PART * part) * 64 + r * 8
                ys[0, row : row + 8, :] = prim[f, pl.ds(base + 16, 8, stride=64), :]
                ys[1, row : row + 8, :] = prim[f, pl.ds(base + 39, 8, stride=64), :]
                for side, at in ((0, 0), (1, 3)):
                    if part == at:
                        row, base = f * 64 + r * 32, (2 + 30 * side + r) * 64 + 16
                        xs[side, row : row + 32, :] = prim[f, base : base + 32, :]
        return halo_copies(part)

    def start_part(part):
        for c in rest[part]:
            c.wait_recv()
        first = part * PART
        assemble((1, 2, 3, 4), first, PART, 2)
        lax.fori_loop(first, first + PART, primitives, 0)
        for c in send_halo(part):
            c.start()
        neighbours_z(part, 0)
        lax.fori_loop(first, first + PART, sweep_z, 0)

    modes = lax.dot_general(
        bz[...], cons[0], (((1,), (1,)), ((), ())),
        precision=HIGHEST, preferred_element_type=jnp.float32,
    )
    for r in range(16):
        for c in range(8):
            spec_t[r, 8 * c : 8 * c + 8, :] = modes[8 * r : 8 * r + 8, 128 * c : 128 * c + 128]

    def a2a_copy(peer, source):
        return send(
            spec_t.at[pl.ds(2 * peer, 2)], spec_r.at[pl.ds(2 * source, 2)],
            A2A + peer, {"gx": peer}, A2A + source,
        )

    def start_a2a(o, _):
        a2a_copy((g + o) % NG, g).start()
        return 0

    lax.fori_loop(1, NG, start_a2a, 0)
    for c in rest[1]:
        c.start()
    spec_r[pl.ds(2 * g, 2)] = spec_t[pl.ds(2 * g, 2)]
    start_part(0)
    for c in rest[2]:
        c.start()
    start_part(1)

    def wait_a2a(o, _):
        source = (g + NG - o) % NG
        a2a_copy(source, source).wait_recv()
        return 0

    lax.fori_loop(1, NG, wait_a2a, 0)
    for c in rest[3]:
        c.start()

    def to_lines(r, _):
        for q in range(2):
            parts = [spec_r[r, pl.ds(4 * q + b, 8, stride=8), :] for b in range(4)]
            for i, v in enumerate(swap4(parts)):
                lines[at8(r * 32 + 8 * i), 128 * q : 128 * q + 128] = v
        return 0

    lax.fori_loop(0, 16, to_lines, 0)
    lined = lax.dot_general(
        lines[...], sf[...], (((0,), (0,)), ((), ())),
        precision=HIGHEST, preferred_element_type=jnp.float32,
    )
    for t in range(4):
        trans[t] = lined[:, 128 * t : 128 * t + 128]

    k_four, k_in = k // 4, k % 4
    lam, gain = tab[0], tab[1]
    lam2 = lam * lam
    lam4 = lam2 * lam2
    lam8 = lam4 * lam4
    lam16 = lam8 * lam8
    lam32 = lam16 * lam16
    lam64 = lam32 * lam32
    lam128 = lam64 * lam64

    def line_rows(y):
        return pl.ds((y % 4) * 8 + y // 4, 8, stride=32)

    def line(y):
        return jnp.concatenate([trans[t, line_rows(y), :] for t in range(4)], axis=1)

    def sums(i, carry):
        u, v = carry
        low, high = line(i), line(31 - i)
        held[i] = low
        return low + lam * u, high + lam * v

    zero = jnp.zeros((8, 512), jnp.float32)
    up_sum, down_sum = lax.fori_loop(0, 32, sums, (zero, zero))
    mom_z[k_in, 0:8, :] = up_sum
    mom_z[k_in, 8:16, :] = down_sum

    def mom_z_copy(peer, source):
        return send(
            mom_z.at[source], mom_z.at[source], MOM_Z + peer, {"gy": 4 * k_four + peer}, MOM_Z + source
        )

    def mom_y_copy(peer, source):
        return send(
            mom_y.at[source], mom_y.at[source], MOM_Y + peer, {"gy": 4 * peer + k_in}, MOM_Y + source
        )

    for o in range(1, 4):
        mom_z_copy((k_in + o) % 4, k_in).start()
    start_part(2)
    for o in range(1, 4):
        source = (k_in + 4 - o) % 4
        mom_z_copy(source, source).wait_recv()
    from_low, from_high, four_up, four_down = zero, zero, zero, zero
    power_low, power_high = zero + 1.0, zero + 1.0
    for i in range(4):
        ups, downs = mom_z[i, 0:8, :], mom_z[3 - i, 8:16, :]
        four_up = four_up * lam32 + ups
        four_down = four_down * lam32 + downs
        from_low = jnp.where(i < k_in, from_low * lam32 + ups, from_low)
        from_high = jnp.where(3 - i > k_in, from_high * lam32 + downs, from_high)
        power_low = jnp.where(i < k_in, power_low * lam32, power_low)
        power_high = jnp.where(3 - i > k_in, power_high * lam32, power_high)
    mom_y[k_four, 0:8, :] = four_up
    mom_y[k_four, 8:16, :] = four_down
    for o in range(1, 4):
        mom_y_copy((k_four + o) % 4, k_four).start()
    start_part(3)
    for o in range(1, 4):
        source = (k_four + 4 - o) % 4
        mom_y_copy(source, source).wait_recv()

    far_low, far_high, at_start, at_end = zero, zero, zero, zero
    far_power_low, far_power_high = zero + 1.0, zero + 1.0
    for i in range(4):
        ups, downs = mom_y[i, 0:8, :], mom_y[3 - i, 8:16, :]
        at_end = at_end * lam128 + ups
        at_start = at_start * lam128 + downs
        far_low = jnp.where(i < k_four, far_low * lam128 + ups, far_low)
        far_high = jnp.where(3 - i > k_four, far_high * lam128 + downs, far_high)
        far_power_low = jnp.where(i < k_four, far_power_low * lam128, far_power_low)
        far_power_high = jnp.where(3 - i > k_four, far_power_high * lam128, far_power_high)
    lam256 = lam128 * lam128
    whole = lam256 * lam256 * lam
    at_start, at_end = lam * at_start, lam * at_end
    scale = 1.0 / (1.0 - whole * whole)
    low_image = (at_start - whole * at_end) * scale * far_power_low
    high_image = (at_end - whole * at_start) * scale * far_power_high
    first_u = from_low + power_low * (far_low - low_image)
    first_v = from_high + power_high * (far_high - high_image)

    def downward(i, v):
        v = held[31 - i] + lam * v
        vsol[31 - i] = v
        return v

    lax.fori_loop(0, 32, downward, first_v)

    def upward(i, u):
        carried = lam * u
        f = held[i]
        value = gain * (carried + vsol[i])
        for t in range(4):
            trans[t, line_rows(i), :] = value[:, 128 * t : 128 * t + 128]
        return f + carried

    lax.fori_loop(0, 32, upward, first_u)
    lines[...] = lax.dot_general(
        si[...], jnp.concatenate([trans[t] for t in range(4)], axis=1), (((1,), (1,)), ((), ())),
        precision=HIGHEST, preferred_element_type=jnp.float32,
    )

    def from_lines(r, _):
        for q in range(2):
            parts = [lines[at8(r * 32 + 8 * i), 128 * q : 128 * q + 128] for i in range(4)]
            for b, v in enumerate(swap4(parts)):
                back_t[r, pl.ds(4 * q + b, 8, stride=8), :] = v
        return 0

    lax.fori_loop(0, 16, from_lines, 0)

    def back_copy(peer, source):
        return send(
            back_t.at[pl.ds(2 * peer, 2)], back_r.at[pl.ds(2 * source, 2)],
            BACK + peer, {"gx": peer}, BACK + source,
        )

    def start_back(o, _):
        back_copy((g + o) % NG, g).start()
        return 0

    lax.fori_loop(1, NG, start_back, 0)
    back_r[pl.ds(2 * g, 2)] = back_t[pl.ds(2 * g, 2)]


    def place_halo_x():
        for c in halo_x:
            c.wait_recv()
        for f in range(5):
            for r in range(2):
                for j in range(4):
                    row = f * 64 + r * 32 + j * 8
                    e = (j + 2) * 8

                    def plane(xx):
                        return prim[f, (xx + 2) * 64 + e : (xx + 2) * 64 + e + 8, :]

                    low = pltpu.roll(jnp.where(lane >= 64, xr[0, row : row + 8, :], plane(30 + r)), 64, 1)
                    low = jnp.where((lane < 64) & (g == 0), plane(0), low)
                    prim[f, r * 64 + e : r * 64 + e + 8, :] = low
                    high = pltpu.roll(jnp.where(lane < 64, xr[1, row : row + 8, :], plane(r)), 64, 1)
                    high = jnp.where((lane >= 64) & (g == NG - 1), plane(31), high)
                    prim[f, (34 + r) * 64 + e : (34 + r) * 64 + e + 8, :] = high

    def place_y(x, _):
        base = (x + 2) * 64
        for f in range(5):
            rows = [prim[f, at8(base + 16 + 8 * j), :] for j in range(4)]
            first = jnp.broadcast_to(rows[0][0:1, :], (8, 128))
            final = jnp.broadcast_to(rows[3][7:8, :], (8, 128))
            for r in range(2):
                row = (x // PART) * 80 + f * 16 + r * 8 + x % PART
                low = jnp.where(k == 0, first, jnp.broadcast_to(yr[0, pl.ds(row, 1), :], (8, 128)))
                prim[f, at8(base + 8 * r), :] = jnp.where(sub == 0, low, pltpu.roll(rows[2 + r], 1, 0))
                high = jnp.where(k == NK - 1, final, jnp.broadcast_to(yr[1, pl.ds(row, 1), :], (8, 128)))
                prim[f, at8(base + 48 + 8 * r), :] = jnp.where(sub == 7, high, pltpu.roll(rows[r], 7, 0))
        return 0

    def place_halo_y(part):
        for c in halo_y(part):
            c.wait_recv()
        lax.fori_loop(PART * part, PART * part + PART, place_y, 0)

    def sweep_row(cell, count, normal, target):
        before_left, before_flux = None, None
        for i in range(-1, count + 1):
            left, right = [], []
            for f in range(5):
                v = cell(f, i)
                h = half_slope(v - cell(f, i - 1), cell(f, i + 1) - v)
                left.append(v + h)
                right.append(v - h)
            if before_left is not None:
                flux = face_flux(before_left, right, normal)
                if before_flux is not None:
                    for f in range(5):
                        row = target(i - 1)
                        acc[f, row, :] = acc[f, row, :] + (flux[f] - before_flux[f])
                before_flux = flux
            before_left = left

    def hydro(part):
        def sweep_y(i, _):
            x = part * PART + i
            base = (x + 2) * 64 + 16
            sweep_row(
                lambda f, e: prim[f, at8(base + 8 * e), :], 4, 1, lambda e: at8(x * 32 + 8 * e)
            )
            return 0

        lax.fori_loop(0, PART, sweep_y, 0)

        def sweep_x(j, _):
            base = (part * PART + 2) * 64 + 16 + 8 * j
            sweep_row(
                lambda f, i: prim[f, at8(base + 64 * i), :], PART, 0,
                lambda i: at8((part * PART + i) * 32 + 8 * j),
            )
            return 0

        lax.fori_loop(0, 4, sweep_x, 0)

    def finish(part):
        def body(i, _):
            x = part * PART + i
            base = (x + 1) * 48 + 8
            new = [[None] * 4 for _ in range(4)]
            half = -0.5 * dt
            for j in range(4):
                ax = half * (pot[at8(base + 48 + 8 * j), :] - pot[at8(base - 48 + 8 * j), :])
                ay = half * (pot[at8(base + 8 + 8 * j), :] - pot[at8(base - 8 + 8 * j), :])
                az = half * potz[at8(x * 32 + 8 * j), :]
                u = [cons[f, at8(x * 32 + 8 * j), :] for f in range(5)]
                change = [acc[f, at8(x * 32 + 8 * j), :] for f in range(5)]
                for i3, a in enumerate((ax, ay, az)):
                    new[i3][j] = u[1 + i3] - dt * change[1 + i3] + u[0] * a
                new[3][j] = u[4] - dt * change[4] + (u[1] * ax + u[2] * ay + u[3] * az)
            for f in range(4):
                b0, b2, b1, b3 = swap4(new[f])
                for q, v in enumerate((b0, b1, b2, b3)):
                    nb[1 + q, 1 + f, x] = v
            return 0

        lax.fori_loop(0, PART, body, 0)

    def after_copies(part):
        fields, span = pl.ds(1, 4), pl.ds(part * PART, PART)
        return [
            send(nb.at[1, fields, span], nb.at[5, fields, span], AFTER + part, {"gy": k_dn}),
            send(nb.at[4, fields, span], nb.at[0, fields, span], AFTER + 4 + part, {"gy": k_up}),
        ]

    def emit(part):
        for c in after_copies(part):
            c.start()

    def deficit(x, total):
        for j in range(4):
            row = at8(x * 32 + 8 * j)
            density = cons[0, row, :] - dt * acc[0, row, :]
            total = total + (jnp.maximum(density, FLOOR) - density)
        return total

    def def_copy(peer, source):
        return send(defs.at[source], defs.at[source], DEF_Y + peer, {"gy": peer}, DEF_Y + source)

    def start_def(o, _):
        def_copy((k + o) % NK, k).start()
        return 0

    def wait_def(o, _):
        source = (k + NK - o) % NK
        def_copy(source, source).wait_recv()
        return 0

    def density_copies(part):
        span = pl.ds(part * PART, PART)
        return [
            send(nb.at[1, 0, span], nb.at[5, 0, span], DENSITY + part, {"gy": k_dn}),
            send(nb.at[4, 0, span], nb.at[0, 0, span], DENSITY + 4 + part, {"gy": k_up}),
        ]

    def finish_density(part):
        def body(i2, _):
            for i in range(2):
                x = part * PART + i2 * 2 + i
                new = []
                for j in range(4):
                    row = at8(x * 32 + 8 * j)
                    new.append(jnp.maximum(cons[0, row, :] - dt * acc[0, row, :], FLOOR))
                b0, b2, b1, b3 = swap4(new)
                for q, v in enumerate((b0, b1, b2, b3)):
                    nb[1 + q, 0, x] = v
            return 0

        lax.fori_loop(0, PART // 2, body, 0)
        for c in density_copies(part):
            c.start()

    place_halo_y(1)
    hydro(1)
    finish_density(1)
    place_halo_y(2)
    hydro(2)
    finish_density(2)

    def wait_back(o, _):
        source = (g + NG - o) % NG
        back_copy(source, source).wait_recv()
        return 0

    lax.fori_loop(1, NG, wait_back, 0)
    both = lax.dot_general(
        jnp.concatenate(
            [
                jnp.concatenate([back_r[r, 8 * c : 8 * c + 8, :] for c in range(8)], axis=1)
                for r in range(16)
            ]
        ),
        bzi[...], (((0,), (0,)), ((), ())),
        precision=HIGHEST, preferred_element_type=jnp.float32,
    )
    pot0[...] = both[:, 0:128]
    potz[...] = both[:, 128:256]
    pxs[0] = pot0[0:32, :]
    pxs[1] = pot0[31 * 32 : 32 * 32, :]
    for q in range(4):
        pys[0, 8 * q : 8 * q + 8, :] = pot0[pl.ds(8 * q * 32, 8, stride=32), :]
        pys[1, 8 * q : 8 * q + 8, :] = pot0[pl.ds(8 * q * 32 + 31, 8, stride=32), :]
    phi_halo = [
        send(pxs.at[0], pxr.at[1], PHI, {"gx": g_dn}),
        send(pxs.at[1], pxr.at[0], PHI + 1, {"gx": g_up}),
        send(pys.at[0], pyr.at[1], PHI + 2, {"gy": k_dn}),
        send(pys.at[1], pyr.at[0], PHI + 3, {"gy": k_up}),
    ]
    for c in phi_halo:
        c.start()

    place_halo_x()
    place_halo_y(0)
    place_halo_y(3)
    hydro(0)
    hydro(3)
    defs[k] = lax.fori_loop(0, 32, deficit, jnp.zeros((8, 128), jnp.float32))
    lax.fori_loop(1, NK, start_def, 0)
    finish_density(0)
    finish_density(3)
    for c in phi_halo:
        c.wait_recv()
    for j in range(4):
        low = pltpu.roll(
            jnp.where(lane >= 64, pxr[0, 8 * j : 8 * j + 8, :], pot0[31 * 32 + 8 * j : 31 * 32 + 8 * j + 8, :]), 64, 1
        )
        pot[8 + 8 * j : 16 + 8 * j, :] = jnp.where((lane < 64) & (g == 0), 0.0, low)
        high = pltpu.roll(jnp.where(lane < 64, pxr[1, 8 * j : 8 * j + 8, :], pot0[8 * j : 8 * j + 8, :]), 64, 1)
        pot[33 * 48 + 8 + 8 * j : 33 * 48 + 16 + 8 * j, :] = jnp.where((lane >= 64) & (g == NG - 1), 0.0, high)

    def place_pot(x, _):
        base = (x + 1) * 48
        rows = [pot0[at8(x * 32 + 8 * j), :] for j in range(4)]
        for j in range(4):
            pot[at8(base + 8 + 8 * j), :] = rows[j]
        low = jnp.where(k == 0, 0.0, jnp.broadcast_to(pyr[0, pl.ds(x, 1), :], (8, 128)))
        pot[at8(base), :] = jnp.where(sub == 0, low, pltpu.roll(rows[3], 1, 0))
        high = jnp.where(k == NK - 1, 0.0, jnp.broadcast_to(pyr[1, pl.ds(x, 1), :], (8, 128)))
        pot[at8(base + 40), :] = jnp.where(sub == 7, high, pltpu.roll(rows[0], 7, 0))
        return 0

    lax.fori_loop(0, 32, place_pot, 0)
    def finish_part(part):
        finish(part)
        emit(part)

    finish_part(1)
    finish_part(2)
    lax.fori_loop(1, NK, wait_def, 0)
    dgx[g] = jnp.sum(defs[...], axis=0)

    def dgx_copy(peer, source):
        return send(dgx.at[source], dgx.at[source], DEF_X + peer, {"gx": peer}, DEF_X + source)

    def start_dgx(o, _):
        dgx_copy((g + o) % NG, g).start()
        return 0

    def wait_dgx(o, _):
        source = (g + NG - o) % NG
        dgx_copy(source, source).wait_recv()
        return 0

    lax.fori_loop(1, NG, start_dgx, 0)
    for part in (0, 3):
        finish_part(part)
    lax.fori_loop(1, NG, wait_dgx, 0)
    added[0, 0] = jnp.sum(jnp.sum(dgx[...], axis=0)) * (1.0 / 512)

    halo = sum([halo_copies(part) for part in range(32 // PART)], [])
    for c in edges + sum(rest, []) + halo + phi_halo:
        c.wait_send()

    def sent_y(o, _):
        def_copy((k + o) % NK, k).wait_send()
        return 0

    def sent_x(o, _):
        peer = (g + o) % NG
        a2a_copy(peer, g).wait_send()
        back_copy(peer, g).wait_send()
        dgx_copy(peer, g).wait_send()
        return 0

    for o in range(1, 4):
        mom_z_copy((k_in + o) % 4, k_in).wait_send()
        mom_y_copy((k_four + o) % 4, k_four).wait_send()
    lax.fori_loop(1, NK, sent_y, 0)
    lax.fori_loop(1, NG, sent_x, 0)
    for part in range(32 // PART):
        for c in density_copies(part) + after_copies(part):
            c.wait()


def place_kernel(after, where, nb, out, tmp, ready, sem):
    g, k = where[0], where[1]
    begin = after[g, k]
    end = jnp.where(k < NK - 1, after[g, jnp.minimum(k + 1, NK - 1)], 4 * NK)
    lead, held = jnp.clip(begin - 4 * k, -1, 1), end - begin
    writes = [pltpu.make_async_copy(ready.at[f], out.at[f], sem.at[f]) for f in range(5)]
    for f in range(5):

        def body(x4, _):
            for i4 in range(4):
                x = x4 * 4 + i4
                for slot in range(6):
                    index = jnp.minimum(slot + lead + 1, 5)
                    v = jnp.where(slot < held, nb[index, f, x], 0.0)
                    tmp[i4, pl.ds(slot, 8, stride=8), :] = v
                for s in range(8):
                    ready[f, :, pl.ds(pl.multiple_of(x * 1024 + 128 * s, 128), 128)] = tmp[i4, 8 * s : 8 * s + 6, :]
            return 0

        lax.fori_loop(0, 8, body, 0)
        writes[f].start()
    for c in writes:
        c.wait()


def per_device(consts, state_before, before_start, after_start, time_step):
    f32 = jnp.float32
    st = jnp.transpose(state_before, (1, 0, 2))
    any_spec = pl.BlockSpec(memory_space=pl.ANY)
    smem = pl.BlockSpec(memory_space=pltpu.SMEM)
    vmem = pl.BlockSpec(memory_space=pltpu.VMEM)
    block = (5, 32, 8, 128)

    def scratch(*shape):
        return pltpu.VMEM(shape, f32)

    nb, added = pl.pallas_call(
        step_kernel,
        out_shape=(pltpu.VMEM((6,) + block, f32), jax.ShapeDtypeStruct((1, 1), f32)),
        in_specs=[any_spec, smem, smem] + [any_spec] * 6,
        out_specs=(vmem, smem),
        scratch_shapes=[
            scratch(5, 6, 32768),
            scratch(4, 64, 128),
            scratch(6, *block),
            scratch(*block),
            scratch(*block),
            scratch(*block),
            scratch(5, 1024, 128),
            scratch(5, 36 * 64, 128),
            scratch(5, 1024, 128),
            scratch(5, 1024, 128), scratch(5, 1024, 128),
            scratch(34 * 48, 128),
            scratch(1024, 128),
            scratch(1024, 128),
            scratch(2, 320, 128), scratch(2, 320, 128), scratch(2, 320, 128), scratch(2, 320, 128),
            scratch(2, 32, 128), scratch(2, 32, 128), scratch(2, 32, 128), scratch(2, 32, 128),
            scratch(16, 64, 128),
            scratch(16, 64, 128),
            scratch(512, 256),
            scratch(4, 256, 128),
            scratch(32, 8, 512),
            scratch(32, 8, 512),
            scratch(16, 64, 128),
            scratch(16, 64, 128),
            scratch(4, 16, 512),
            scratch(4, 16, 512),
            scratch(16, 8, 128),
            scratch(8, 8, 128),
            scratch(128, 128), scratch(128, 256), scratch(512, 512), scratch(512, 512),
            scratch(2, 8, 512),
            pltpu.VMEM((256, 256), jnp.bfloat16),
            pltpu.SemaphoreType.DMA((11,)),
            pltpu.SemaphoreType.DMA((N_SEM,)),
            pltpu.SemaphoreType.DMA((N_SEM,)),
        ],
        compiler_params=pltpu.CompilerParams(
            collective_id=0, has_side_effects=True, vmem_limit_bytes=58 * 1024 * 1024
        ),
        name="step",
    )(st, before_start, time_step.reshape(1, 1), *consts)

    where = jnp.stack([lax.axis_index("gx"), lax.axis_index("gy")]).astype(jnp.int32)
    out = pl.pallas_call(
        place_kernel,
        out_shape=jax.ShapeDtypeStruct((5, 6, 32768), f32),
        in_specs=[smem, smem, vmem],
        out_specs=any_spec,
        scratch_shapes=[
            scratch(4, 64, 128), scratch(5, 6, 32768), pltpu.SemaphoreType.DMA((5,)),
        ],
        compiler_params=pltpu.CompilerParams(vmem_limit_bytes=32 * 1024 * 1024),
        name="place",
    )(after_start, where, nb)
    return jnp.transpose(out, (1, 0, 2)), added.reshape(())


def solution(mesh):
    consts = tables()

    def run(*args):
        return per_device([jnp.asarray(c) for c in consts[:-1]] + [jnp.asarray(consts[-1], jnp.bfloat16)], *args)

    placed = (P(("gx", "gy"), None, None), P(), P(), P())
    return jax.shard_map(
        run,
        mesh=mesh,
        in_specs=placed,
        out_specs=(P(("gx", "gy"), None, None), P()),
        check_vma=False,
    )
```

time: 86.9 us -> 80.1 us (0.922)
  the two profiles are of different devices: /device:TPU:8 before, /device:TPU:1 now
where the time goes in v2:
time: 80.1 us; the launch traced here: 79.9 us
  Pallas kernels  76.8 us (96%)
  between operations  3.08 us (4%)
    pallas_call x1, Pallas kernels, per_device(): pl.pallas_call(step_kernel, out_shape=(pltpu.VMEM((6,) + block, f32), jax...  73 us
    pallas_call x1, Pallas kernels, per_device(): pl.pallas_call(place_kernel, out_shape=jax.ShapeDtypeStruct((5, 6, 32768)...  3.83 us

profile of v2, /device:TPU:1, one launch (start us, length us, event | category | flops | bytes accessed | tf_op | source)
XLA Modules:
  0.0 79.9 jit_solution(11766761918703103633)
XLA Ops:
  0.6 0.0 copy-start
  1.3 0.1 pad_add_fusion.where
  1.4 73.0 %step.1 = (f32[6,5,32,8,128]{4,3,2,1,0:T(8,128)S(1)}, f32[1,1]{1,0:T(1,128)}) custom-call(f32[5,6,32768]{2,1,0:T(8,128)} %bitcast.7, s32[8,16]{1,0:T(8,128)} %before.1, f32[1,1]{1,0:T(1,128)} %bitcast.6.dt_ref, f32[128,128]{1,0:T(8,128)} %constant.21.clone.bz_h, f32[128,256]{1,0:T(8,128)} %constant.22.clone.bzi_h, f32[512,512]{1,0:T(8,128)} %constant.23.clone.sf_h, ...), custom_call_target="tpu_custom_call" | custom-call | tf_op jit(solution)/shard_map/step/pallas_call | solution.py:806
  74.3 0.0 copy-done
  74.4 3.8 %place.1 = f32[5,6,32768]{2,1,0:T(8,128)} custom-call(s32[8,16]{1,0:T(8,128)S(1)} %copy-done, s32[2]{0:T(128)S(1)} %pad_add_fusion.where, f32[6,5,32,8,128]{4,3,2,1,0:T(8,128)S(1)} %get-tuple-element.4.nb), custom_call_target="tpu_custom_call" | custom-call | tf_op jit(solution)/shard_map/place/pallas_call | solution.py:853
Async XLA Ops:
  0.6 73.7 %copy-start = (s32[8,16]{1,0:T(8,128)S(1)}, s32[8,16]{1,0:T(8,128)}, u32[]{:S(2)}) copy-start(s32[8,16]{1,0:T(8,128)} %after.1) | copy-start | bytes 1540

commit v3 on v2

--- a/solution.py
+++ b/solution.py
@@ -651,6 +651,10 @@
     place_halo_y(2)
     hydro(2)
     finish_density(2)
+    place_halo_x()
+    place_halo_y(3)
+    hydro(3)
+    finish_density(3)
 
     def wait_back(o, _):
         source = (g + NG - o) % NG
@@ -684,15 +688,11 @@
     for c in phi_halo:
         c.start()
 
-    place_halo_x()
     place_halo_y(0)
-    place_halo_y(3)
     hydro(0)
-    hydro(3)
     defs[k] = lax.fori_loop(0, 32, deficit, jnp.zeros((8, 128), jnp.float32))
     lax.fori_loop(1, NK, start_def, 0)
     finish_density(0)
-    finish_density(3)
     for c in phi_halo:
         c.wait_recv()
     for j in range(4):
@@ -772,7 +772,12 @@
     begin = after[g, k]
     end = jnp.where(k < NK - 1, after[g, jnp.minimum(k + 1, NK - 1)], 4 * NK)
     lead, held = jnp.clip(begin - 4 * k, -1, 1), end - begin
-    writes = [pltpu.make_async_copy(ready.at[f], out.at[f], sem.at[f]) for f in range(5)]
+    halves = [pl.ds(0, 16384), pl.ds(16384, 16384)]
+    writes = [
+        pltpu.make_async_copy(ready.at[f, :, h], out.at[f, :, h], sem.at[2 * f + i])
+        for f in range(5)
+        for i, h in enumerate(halves)
+    ]
     for f in range(5):
 
         def body(x4, _):
@@ -786,8 +791,9 @@
                     ready[f, :, pl.ds(pl.multiple_of(x * 1024 + 128 * s, 128), 128)] = tmp[i4, 8 * s : 8 * s + 6, :]
             return 0
 
-        lax.fori_loop(0, 8, body, 0)
-        writes[f].start()
+        for i in range(2):
+            lax.fori_loop(4 * i, 4 * i + 4, body, 0)
+            writes[2 * f + i].start()
     for c in writes:
         c.wait()
 
@@ -856,7 +862,7 @@
         in_specs=[smem, smem, vmem],
         out_specs=any_spec,
         scratch_shapes=[
-            scratch(4, 64, 128), scratch(5, 6, 32768), pltpu.SemaphoreType.DMA((5,)),
+            scratch(4, 64, 128), scratch(5, 6, 32768), pltpu.SemaphoreType.DMA((10,)),
         ],
         compiler_params=pltpu.CompilerParams(vmem_limit_bytes=32 * 1024 * 1024),
         name="place",

time: 80.1 us -> 76.7 us (0.958); the launches traced: 79.9 us -> 75.6 us
  Pallas kernels: 76.8 us -> 72.5 us
    pallas_call x1, Pallas kernels: 73 us -> 68.8 us  [per_device(): pl.pallas_call(step_kernel, out_shape=(pltpu.VMEM((6,) + block, f32), jax...]
where the time goes in v3:
time: 76.7 us; the launch traced here: 75.6 us
  Pallas kernels  72.5 us (95%)
  between operations  3.08 us (4%)
    pallas_call x1, Pallas kernels, per_device(): pl.pallas_call(step_kernel, out_shape=(pltpu.VMEM((6,) + block, f32), jax...  68.8 us
    pallas_call x1, Pallas kernels, per_device(): pl.pallas_call(place_kernel, out_shape=jax.ShapeDtypeStruct((5, 6, 32768)...  3.64 us

profile of v3, /device:TPU:1, one launch (start us, length us, event | category | flops | bytes accessed | tf_op | source)
XLA Modules:
  0.0 75.6 jit_solution(9903844283202340038)
XLA Ops:
  0.6 0.0 copy-start
  1.3 0.1 pad_add_fusion.where
  1.4 68.8 %step.1 = (f32[6,5,32,8,128]{4,3,2,1,0:T(8,128)S(1)}, f32[1,1]{1,0:T(1,128)}) custom-call(f32[5,6,32768]{2,1,0:T(8,128)} %bitcast.7, s32[8,16]{1,0:T(8,128)} %before.1, f32[1,1]{1,0:T(1,128)} %bitcast.6.dt_ref, f32[128,128]{1,0:T(8,128)} %constant.21.clone.bz_h, f32[128,256]{1,0:T(8,128)} %constant.22.clone.bzi_h, f32[512,512]{1,0:T(8,128)} %constant.23.clone.sf_h, ...), custom_call_target="tpu_custom_call" | custom-call | tf_op jit(solution)/shard_map/step/pallas_call | solution.py:812
  70.2 0.0 copy-done
  70.2 3.6 %place.1 = f32[5,6,32768]{2,1,0:T(8,128)} custom-call(s32[8,16]{1,0:T(8,128)S(1)} %copy-done, s32[2]{0:T(128)S(1)} %pad_add_fusion.where, f32[6,5,32,8,128]{4,3,2,1,0:T(8,128)S(1)} %get-tuple-element.4.nb), custom_call_target="tpu_custom_call" | custom-call | tf_op jit(solution)/shard_map/place/pallas_call | solution.py:859
Async XLA Ops:
  0.6 69.6 %copy-start = (s32[8,16]{1,0:T(8,128)S(1)}, s32[8,16]{1,0:T(8,128)}, u32[]{:S(2)}) copy-start(s32[8,16]{1,0:T(8,128)} %after.1) | copy-start | bytes 1540

commit v4 on v3

--- a/solution.py
+++ b/solution.py
@@ -358,7 +358,7 @@
                 lines[at8(r * 32 + 8 * i), 128 * q : 128 * q + 128] = v
         return 0
 
-    lax.fori_loop(0, 16, to_lines, 0)
+    lax.fori_loop(0, 16, to_lines, 0, unroll=2)
     lined = lax.dot_general(
         lines[...], sf[...], (((0,), (0,)), ((), ())),
         precision=HIGHEST, preferred_element_type=jnp.float32,
@@ -382,14 +382,16 @@
     def line(y):
         return jnp.concatenate([trans[t, line_rows(y), :] for t in range(4)], axis=1)
 
-    def sums(i, carry):
-        u, v = carry
-        low, high = line(i), line(31 - i)
-        held[i] = low
-        return low + lam * u, high + lam * v
+    def sum_up(i, u):
+        held[i] = line(i)
+        return held[i] + lam * u
+
+    def sum_down(i, v):
+        return held[31 - i] + lam * v
 
     zero = jnp.zeros((8, 512), jnp.float32)
-    up_sum, down_sum = lax.fori_loop(0, 32, sums, (zero, zero))
+    up_sum = lax.fori_loop(0, 32, sum_up, zero)
+    down_sum = lax.fori_loop(0, 32, sum_down, zero)
     mom_z[k_in, 0:8, :] = up_sum
     mom_z[k_in, 8:16, :] = down_sum
 
@@ -475,7 +477,7 @@
                 back_t[r, pl.ds(4 * q + b, 8, stride=8), :] = v
         return 0
 
-    lax.fori_loop(0, 16, from_lines, 0)
+    lax.fori_loop(0, 16, from_lines, 0, unroll=2)
 
     def back_copy(peer, source):
         return send(

time: 76.7 us -> 76.8 us (level); the launches traced: 75.6 us -> 76.6 us
  Pallas kernels: 72.5 us -> 73.4 us
    pallas_call x1, Pallas kernels: 68.8 us -> 69.8 us  [per_device(): pl.pallas_call(step_kernel, out_shape=(pltpu.VMEM((6,) + block, f32), jax...]
where the time goes in v4:
time: 76.8 us; the launch traced here: 76.6 us
  Pallas kernels  73.4 us (96%)
  between operations  3.08 us (4%)
    pallas_call x1, Pallas kernels, per_device(): pl.pallas_call(step_kernel, out_shape=(pltpu.VMEM((6,) + block, f32), jax...  69.8 us
    pallas_call x1, Pallas kernels, per_device(): pl.pallas_call(place_kernel, out_shape=jax.ShapeDtypeStruct((5, 6, 32768)...  3.64 us

profile of v4, /device:TPU:1, one launch (start us, length us, event | category | flops | bytes accessed | tf_op | source)
XLA Modules:
  0.0 76.6 jit_solution(2132462324872441676)
XLA Ops:
  0.6 0.0 copy-start
  1.3 0.1 pad_add_fusion.where
  1.4 69.8 %step.1 = (f32[6,5,32,8,128]{4,3,2,1,0:T(8,128)S(1)}, f32[1,1]{1,0:T(1,128)}) custom-call(f32[5,6,32768]{2,1,0:T(8,128)} %bitcast.7, s32[8,16]{1,0:T(8,128)} %before.1, f32[1,1]{1,0:T(1,128)} %bitcast.6.dt_ref, f32[128,128]{1,0:T(8,128)} %constant.21.clone.bz_h, f32[128,256]{1,0:T(8,128)} %constant.22.clone.bzi_h, f32[512,512]{1,0:T(8,128)} %constant.23.clone.sf_h, ...), custom_call_target="tpu_custom_call" | custom-call | tf_op jit(solution)/shard_map/step/pallas_call | solution.py:814
  71.2 0.0 copy-done
  71.2 3.6 %place.1 = f32[5,6,32768]{2,1,0:T(8,128)} custom-call(s32[8,16]{1,0:T(8,128)S(1)} %copy-done, s32[2]{0:T(128)S(1)} %pad_add_fusion.where, f32[6,5,32,8,128]{4,3,2,1,0:T(8,128)S(1)} %get-tuple-element.4.nb), custom_call_target="tpu_custom_call" | custom-call | tf_op jit(solution)/shard_map/place/pallas_call | solution.py:861
Async XLA Ops:
  0.6 70.5 %copy-start = (s32[8,16]{1,0:T(8,128)S(1)}, s32[8,16]{1,0:T(8,128)}, u32[]{:S(2)}) copy-start(s32[8,16]{1,0:T(8,128)} %after.1) | copy-start | bytes 1540
